TPU v7x, 512 devices: a whole 4x4x16 slice. The times are simulated.
512 devices in a mesh: ctx: 32 (over z, core), inner: 16 (over y, x).
Axes of the slice: x: 4, y: 4, z: 16, core: 2. Of those that a mesh axis runs over, the one named last changes fastest.
Arguments:
- tokens: bfloat16 [65536, 2048], P(('ctx', 'inner')), may hold values from -6 to 6
- project_weight: bfloat16 [2048, 2, 4096], P('ctx', None, 'inner'), may hold values from -0.125 to 0.125
- state_weight: bfloat16 [2048, 2, 512], P('ctx', None, 'inner'), may hold values from -0.125 to 0.125
- step_weight: bfloat16 [2048, 64], P('ctx', 'inner'), may hold values from -0.125 to 0.125
- mixer_taps: float32 [5, 4096], P(None, 'inner'), may hold values from -2.5 to 2.5
- state_taps: float32 [5, 2, 512], replicated, may hold values from -2.5 to 2.5
- step_bias: float32 [64], P('inner'), may hold values from -4.6 to -2.3
- decay_log: float32 [64], P('inner'), may hold values from -13 to 0.5, as said below
- norm_gain: float32 [4096], replicated, may hold values from 0.1 to 1.9
Outputs:
- mixed_output: bfloat16 [65536, 4096], P(('ctx', 'inner'))
Inputs may be any that keep to these rules, and one draw needn't show every extreme that they name: `decay_log`: one value a head.
All inputs are finite; a program needn't handle non-finite values.
Results may differ from a plain program's by a relative error of at most 0.0075.
Values may be sent and summed in bfloat16 or wider, within the bound.
A program may use at most 64 MiB of HBM per device.

v0:
```python
import jax
import jax.numpy as jnp
from jax import lax
from jax.sharding import PartitionSpec as P

H = 64
P_SIZE = 64
N = 128
G = 4
CONV = 4
SPAN = 128


EPSILON = 1e-05


def passed_along(x, axis, by):
    count = lax.axis_size(axis)
    pairs = [(i, i + by) for i in range(count) if 0 <= i + by < count]
    return lax.ppermute(x, axis, pairs)


def entering(x, axis, join, neutral):
    place = lax.axis_index(axis)
    gathered = jax.tree.map(
        lambda a, kind: lax.all_gather(a.astype(kind), axis), x, (jnp.bfloat16, jnp.bfloat16)
    )
    state = jax.tree.map(lambda a, e: jnp.zeros_like(a) + jnp.asarray(e, a.dtype), x, neutral)

    def one(turn, state):
        return join(
            state,
            jax.tree.map(
                lambda a, own: lax.dynamic_index_in_dim(a, turn, 0, False).astype(own.dtype),
                gathered,
                x,
            ),
        )

    return lax.fori_loop(0, place, one, state)


def partner(value, axis, stride):
    mask = 2**stride
    pairs = [(source, source ^ mask) for source in range(lax.axis_size(axis))]
    return lax.ppermute(value, axis, pairs)


def conv_apply(taps, previous, current):
    extended = jnp.concatenate([previous, current], axis=0)
    length_rows = current.shape[0]
    mixed = jnp.broadcast_to(taps[CONV], current.shape)
    for offset in range(CONV):
        mixed = mixed + taps[offset] * extended[offset : offset + length_rows].astype(jnp.float32)
    return jax.nn.silu(mixed).astype(jnp.bfloat16)


def join_chain(earlier, later):
    return (earlier[0] + later[0], jnp.exp(later[0])[:, None, None] * earlier[1] + later[1])


def carry_block(state, inputs):
    decay_sum, added = inputs
    return (jnp.exp(decay_sum)[:, None, None] * state + added, state)


def pick_group(values, group):
    shaped = values.reshape(values.shape[:-1] + (N, G))
    return lax.dynamic_index_in_dim(shaped, group, shaped.ndim - 1, keepdims=False)


def on_device(
    tokens,
    project_weight,
    state_weight,
    step_weight,
    mixer_taps,
    state_taps,
    step_bias,
    decay_log,
    norm_gain,
):
    inner_id = lax.axis_index("inner")
    project_rows, state_rows, step_rows = (
        lax.all_gather(project_weight, "ctx", axis=0, tiled=True),
        lax.all_gather(state_weight, "ctx", axis=0, tiled=True),
        lax.all_gather(step_weight, "ctx", axis=0, tiled=True),
    )
    heads_here = step_weight.shape[1]
    width_here = project_weight.shape[2]
    model_width = project_rows.shape[0]
    group = inner_id * heads_here // (H // G)
    full_cols = lax.all_gather(state_rows, "inner", axis=2, tiled=True)
    slice_cols = N
    state_cols = pick_group(full_cols, group)
    state_conv = pick_group(state_taps, group)
    joined = jnp.concatenate(
        [
            project_rows.reshape(model_width, 2 * width_here),
            state_cols.reshape(model_width, 2 * slice_cols),
            step_rows,
        ],
        axis=1,
    )
    projected = jnp.dot(
        lax.all_gather(tokens, "inner", axis=0, tiled=True),
        joined,
        preferred_element_type=jnp.float32,
    ).astype(jnp.bfloat16)
    rows_total = projected.shape[0]
    gate_values = projected[:, :width_here]
    x_pre = projected[:, width_here : 2 * width_here]
    state_pre = projected[:, 2 * width_here : 2 * width_here + 2 * slice_cols].reshape(
        rows_total, 2, slice_cols
    )
    step_raw = projected[:, 2 * width_here + 2 * slice_cols :]
    edge_row = rows_total - (CONV - 1)
    prior_x, prior_state = passed_along((x_pre[edge_row:], state_pre[edge_row:]), "ctx", 1)
    x_vals = conv_apply(mixer_taps, prior_x, x_pre)
    state_vals = conv_apply(state_conv, prior_state, state_pre)
    blocks = rows_total // SPAN
    b_blocks = state_vals[:, 0].reshape(blocks, SPAN, N)
    c_blocks = state_vals[:, 1].reshape(blocks, SPAN, N)
    step_size = jax.nn.softplus(step_raw.astype(jnp.float32) + step_bias)
    step_heads = step_size.T.reshape(heads_here, blocks, SPAN)
    cumul = jnp.cumsum(step_heads * (-jnp.exp(decay_log))[:, None, None], axis=2)
    scores = jnp.einsum("ctn,csn->cts", c_blocks, b_blocks, preferred_element_type=jnp.float32)
    lower = jnp.tril(jnp.ones((SPAN, SPAN), dtype=bool))
    spacing = jnp.where(lower, cumul[..., :, None] - cumul[..., None, :], -jnp.inf)
    mixing = (scores[None] * jnp.exp(spacing) * step_heads[:, :, None, :]).astype(jnp.bfloat16)
    x_blocks = x_vals.reshape(blocks, SPAN, heads_here, P_SIZE)
    diagonal = jnp.einsum("hcts,cshp->cthp", mixing, x_blocks, preferred_element_type=jnp.float32)
    ending = cumul[:, :, -1]
    to_end = jnp.exp(ending[..., None] - cumul) * step_heads
    weighted_b = (b_blocks.astype(jnp.float32)[None] * to_end[..., None]).astype(jnp.bfloat16)
    fresh = jnp.einsum("hcsn,cshp->chnp", weighted_b, x_blocks, preferred_element_type=jnp.float32)
    empty_state = jnp.zeros((heads_here, N, P_SIZE), jnp.float32)
    block_state, local_in = lax.scan(carry_block, empty_state, (ending.T, fresh))
    block_log = jnp.sum(ending, axis=1)
    before_log = (jnp.cumsum(ending, axis=1) - ending).T
    _, prior_block = entering(
        (block_log, block_state), "ctx", join_chain, (jnp.zeros_like(block_log), empty_state)
    )
    state_in = local_in + jnp.exp(before_log)[:, :, None, None] * prior_block[None]
    c_scaled = (c_blocks.astype(jnp.float32)[None] * jnp.exp(cumul)[..., None]).astype(jnp.bfloat16)
    state_high = state_in.astype(jnp.bfloat16)
    state_low = (state_in - state_high.astype(jnp.float32)).astype(jnp.bfloat16)
    offdiag = jnp.einsum(
        "hctn,chnp->cthp", c_scaled, state_high, preferred_element_type=jnp.float32
    )
    offdiag = offdiag + jnp.einsum(
        "hctn,chnp->cthp", c_scaled, state_low, preferred_element_type=jnp.float32
    )
    outputs = (diagonal + offdiag).reshape(rows_total, width_here)
    gated = (outputs * jax.nn.silu(gate_values.astype(jnp.float32))).astype(jnp.bfloat16)
    gated_wide = gated.astype(jnp.float32)
    squares = jnp.sum(gated_wide * gated_wide, axis=1)
    group_devices = H // G // heads_here
    for bit in range(group_devices.bit_length() - 1):
        squares = squares + partner(squares, "inner", bit)
    power = squares[:, None] / (H * P_SIZE // G)
    gain_here = lax.dynamic_slice_in_dim(norm_gain, inner_id * width_here, width_here, 0)
    normed = (gated_wide * lax.rsqrt(power + EPSILON) * gain_here).astype(jnp.bfloat16)
    result = lax.all_to_all(normed, "inner", split_axis=0, concat_axis=1, tiled=True)
    return result


def solution(mesh):
    placed = (
        P(("ctx", "inner"), None),
        P("ctx", None, "inner"),
        P("ctx", None, "inner"),
        P("ctx", "inner"),
        P(None, "inner"),
        P(),
        P("inner"),
        P("inner"),
        P(),
    )
    return jax.shard_map(
        on_device, mesh=mesh, in_specs=placed, out_specs=P(("ctx", "inner"), None), check_vma=False
    )
```

profile of v0, /device:TPU:480, one launch (start us, length us, event | category | flops | bytes accessed | tf_op | source)
XLA Modules:
  0.0 455.8 jit_solution(17512234280697024061)
XLA Ops:
  8.1 30.7 %all_gather.26 = bf16[2048,2,32]{2,1,0:T(2,128)(2,1)S(1)} all-gather(bf16[64,2,32]{2,1,0:T(2,128)(2,1)S(1)} %copy.91), channel_id=1, replica_groups=mesh['ctx'=32,'inner'=16] {'ctx'}, dimensions={0}, use_global_device_ids=true | all-gather | bytes 270336 | tf_op jit(solution)/shard_map/all_gather | solution.py:86
  38.8 1.8 copy.92
  41.4 29.1 %all-gather.2 = bf16[32,64,4]{1,2,0:T(4,128)(2,1)S(1)} all-gather(bf16[1,64,4]{1,2,0:T(4,128)(2,1)S(1)} %bitcast.102), channel_id=1, replica_groups=mesh['ctx'=32,'inner'=16] {'ctx'}, dimensions={0}, use_global_device_ids=true | all-gather | bytes 16896 | tf_op jit(solution)/shard_map/all_gather | solution.py:87
  70.5 1.1 copy.119
  72.8 6.1 %all-gather.8.cloned.1.call-done = bf16[2048,2,256]{2,1,0:T(2,128)(2,1)} async-done(((bf16[64,2,256]{2,1,0:T(2,128)(2,1)}), bf16[2048,2,256]{2,1,0:T(2,128)(2,1)}) %all-gather.8.cloned.1.call-update) | async-done | bytes 2097168 | tf_op jit(solution)/shard_map/all_gather | solution.py:85
  78.9 2.0 copy.123
  81.0 66.3 %all-gather.10.cloned.1.call-done = bf16[2048,2,512]{0,1,2:T(2,128)(2,1)} async-done(((bf16[2048,2,32]{0,1,2:T(2,128)(2,1)}), bf16[2048,2,512]{0,1,2:T(2,128)(2,1)}) %all-gather.10.cloned.1.call-update) | async-done | bytes 4194320 | tf_op jit(solution)/shard_map/all_gather | solution.py:93
  147.3 1.9 constant_dynamic-slice_fusion.2
  149.6 1.3 copy.95
  150.9 85.3 %all-gather.12.cloned.1.call-done = bf16[2048,2048]{1,0:T(8,128)(2,1)} async-done(((bf16[128,2048]{1,0:T(8,128)(2,1)}), bf16[2048,2048]{1,0:T(8,128)(2,1)}) %all-gather.12.cloned.1.call-update) | async-done | bytes 8388624 | tf_op jit(solution)/shard_map/all_gather | solution.py:106
  236.1 10.8 %fusion.12 = bf16[2048,772]{0,1:T(8,128)(2,1)S(1)} fusion(bf16[2048,2048]{1,0:T(8,128)(2,1)} %all-gather.12.cloned.1.call-done, bf16[2048,4]{1,0:T(8,128)(2,1)} %bitcast.92, bf16[2048,256]{1,0:T(8,128)(2,1)} %copy.95, bf16[2048,512]{1,0:T(8,128)(2,1)S(1)} %bitcast.91), kind=kOutput, calls=%fused_computation.21 | convolution fusion | flops 6487072768 | bytes 14712832 | tf_op jit(solution)/shard_map/dot_general | solution.py:105
  247.2 1.4 copy-done.1
  248.8 1.1 reduce_window_sum.22
  250.2 1.9 collective-permute-start
  252.2 2.1 collective-permute-start.1
  254.4 1.4 collective-permute-done
  255.7 2.2 fusion.51
  258.2 2.2 multiply_convert_fusion.7
  260.8 3.9 fusion.26
  264.7 28.8 %while.26 = (s32[]{:T(128)}, f32[4,128,64]{2,1,0:T(8,128)S(1)}, f32[16,4,128,64]{3,2,1,0:T(8,128)}, f32[16,4]{1,0:T(8,128)S(1)}, f32[16,4,128,64]{3,2,1,0:T(8,128)}, /*index=5*/s32[]{:T(128)}, s32[]{:T(128)}) while((s32[]{:T(128)}, f32[4,128,64]{2,1,0:T(8,128)S(1)}, f32[16,4,128,64]{3,2,1,0:T(8,128)}, f32[16,4]{1,0:T(8,128)S(1)}, ...), condition=%wide.region_2.3_spmd.clone, body=%wide.region_1.2_spmd.clone.sunk | while | flops 131075 | bytes 787088 | solution.py:138
  265.5 1.0 bitcast_add_fusion.2
  267.3 1.0 bitcast_add_fusion.2
  269.1 1.0 bitcast_add_fusion.2
  270.9 1.0 bitcast_add_fusion.2
  272.7 1.0 bitcast_add_fusion.2
  274.5 1.0 bitcast_add_fusion.2
  276.3 1.0 bitcast_add_fusion.2
  278.1 1.0 bitcast_add_fusion.2
  279.9 1.0 bitcast_add_fusion.2
  281.8 1.0 bitcast_add_fusion.2
  283.6 1.0 bitcast_add_fusion.2
  285.4 1.0 bitcast_add_fusion.2
  287.2 1.0 bitcast_add_fusion.2
  289.0 1.0 bitcast_add_fusion.2
  290.8 1.0 bitcast_add_fusion.2
  292.5 1.0 bitcast_add_fusion.2
  294.4 1.3 dynamic-slice
  296.8 42.4 %all-reduce = bf16[128]{0:T(256)(128)(2,1)S(1)} all-reduce(bf16[128]{0:T(256)(128)(2,1)S(1)} %dynamic-update-slice), channel_id=2, replica_groups=mesh['ctx'=32,'inner'=16] {'ctx'}, use_global_device_ids=true, to_apply=%add | all-reduce | flops 128 | bytes 512
  340.3 3.3 fusion.18
  343.6 22.2 %all-gather.14.cloned.1.call-done = bf16[128,128,64]{1,2,0:T(8,128)(2,1)} async-done(((bf16[4,128,64]{1,2,0:T(8,128)(2,1)}), bf16[128,128,64]{1,2,0:T(8,128)(2,1)}) %all-gather.14.cloned.1.call-update) | async-done | bytes 2097168 | tf_op jit(solution)/shard_map/all_gather | solution.py:26
  365.8 34.4 %while.25 = (s32[]{:T(128)}, f32[4,128,64]{2,1,0:T(8,128)S(1)}, s32[]{:T(128)}, bf16[32,4]{1,0:T(8,128)(2,1)S(1)}, bf16[32,4,128,64]{2,3,1,0:T(8,128)(2,1)}, /*index=5*/s32[]{:T(128)}, s32[]{:T(128)}, s32[]{:T(128)}) while((s32[]{:T(128)}, f32[4,128,64]{2,1,0:T(8,128)S(1)}, s32[]{:T(128)}, bf16[32,4]{1,0:T(8,128)(2,1)S(1)}, ...), condition=%wide.region_6.7_spmd, body=%wide.region_5.6_spmd.sunk | while | flops 98313 | bytes 589991 | solution.py:40
  365.8 0.9 constant_dynamic-slice_fusion.4
  367.0 0.9 constant_dynamic-slice_fusion.4
  368.1 0.9 constant_dynamic-slice_fusion.4
  370.4 0.9 constant_dynamic-slice_fusion.4
  371.6 0.9 constant_dynamic-slice_fusion.4
  372.7 0.9 constant_dynamic-slice_fusion.4
  373.9 0.9 constant_dynamic-slice_fusion.4
  375.0 0.9 constant_dynamic-slice_fusion.4
  376.2 0.9 constant_dynamic-slice_fusion.4
  377.3 0.9 constant_dynamic-slice_fusion.4
  378.4 0.9 constant_dynamic-slice_fusion.4
  379.6 0.9 constant_dynamic-slice_fusion.4
  380.7 0.9 constant_dynamic-slice_fusion.4
  400.2 5.2 %fusion.15 = f32[16,4,64,128]{3,2,1,0:T(8,128)S(1)} fusion(f32[16,4,128,64]{3,2,1,0:T(8,128)} %get-tuple-element.77, f32[4,16,128]{2,0,1:T(4,128)S(1)} %copy.110, f32[16,128,128]{2,1,0:T(8,128)S(1)} %convert_element_type.135, f32[4,128,64]{2,1,0:T(8,128)S(1)} %get-tuple-element.79, f32[16,4]{1,0:T(8,128)S(1)} %copy.107), kind=kOutput, calls=%fused_computation.22 | convolution fusion | flops 139460608 | bytes 5406976 | tf_op jit(solution)/shard_map/hctn,chnp->cthp/dot_general | solution.py:151
  405.5 2.7 add_bitcast_fusion
  408.2 1.2 copy.113
  409.4 2.4 fusion.23
  411.8 3.4 collective-permute-start.2
  415.2 2.2 collective-permute-done.2
  417.4 4.9 %collective-permute-start.3 = (f32[2048]{0:T(1024)S(1)}, f32[2048]{0:T(1024)S(1)}, u32[]{:S(2)}, u32[]{:S(2)}) collective-permute-start(f32[2048]{0:T(1024)S(1)} %add.124), channel_id=1, source_target_pairs={{0,2},{1,3},{2,0},{3,1},{4,6},{5,7},{6,4},{7,5},{8,10},{9,11},{10,... | collective-permute-start | bytes 24584 | tf_op jit(solution)/shard_map/ppermute | solution.py:46
  423.0 1.4 collective-permute-done.3
  424.8 23.1 %all_to_all.19 = bf16[16,128,256]{1,2,0:T(8,128)(2,1)S(1)} all-to-all(bf16[16,128,256]{1,2,0:T(8,128)(2,1)S(1)} %copy_bitcast_fusion), channel_id=1, replica_groups=mesh['ctx'=32,'inner'=16] {'inner'}, dimensions={0} | all-to-all | bytes 2097152 | tf_op jit(solution)/shard_map/all_to_all | solution.py:164
  448.0 1.3 copy.115
  (201 shorter events, 42.7 us)
Async XLA Ops:
  6.5 34.9 %copy-start.5 = (bf16[64,4]{0,1:T(4,128)(2,1)S(1)}, bf16[64,4]{0,1:T(4,128)(2,1)}, u32[]{:S(2)}) copy-start(bf16[64,4]{0,1:T(4,128)(2,1)} %param.16) | copy-start | bytes 1540
  6.5 65.1 %copy-start.3 = (f32[5,2,512]{2,1,0:T(2,128)S(1)}, f32[5,2,512]{2,1,0:T(2,128)}, u32[]{:S(2)}) copy-start(f32[5,2,512]{2,1,0:T(2,128)} %param.18) | copy-start | bytes 61444
  6.5 72.4 %all-gather.8.cloned.1.call-start = ((), (), s32[]{:S(2)}) async-start(), calls=%async_computation.1 | async-start | bytes 2162688 | tf_op jit(solution)/shard_map/all_gather | solution.py:85
  7.3 140.0 %all-gather.10.cloned.1.call-start = ((), (), s32[]{:S(2)}) async-start(), calls=%async_computation.2 | async-start | bytes 4456448 | tf_op jit(solution)/shard_map/all_gather | solution.py:93
  38.8 34.0 %copy-start.7 = (f32[4]{0:T(128)S(1)}, f32[4]{0:T(128)}, u32[]{:S(2)}) copy-start(f32[4]{0:T(128)} %param.20) | copy-start | bytes 52
  38.8 34.0 %copy-start.4 = (f32[5,256]{1,0:T(8,128)S(1)}, f32[5,256]{1,0:T(8,128)}, u32[]{:S(2)}) copy-start(f32[5,256]{1,0:T(8,128)} %param.17) | copy-start | bytes 15364
  40.6 195.5 %all-gather.12.cloned.1.call-start = ((), (), s32[]{:S(2)}) async-start(), calls=%async_computation.3 | async-start | bytes 8912896 | tf_op jit(solution)/shard_map/all_gather | solution.py:106
  41.3 324.5 %all-gather.14.cloned.1.call-start = ((), (), s32[]{:S(2)}) async-start(), calls=%async_computation.4 | async-start | bytes 2162688 | tf_op jit(solution)/shard_map/all_gather | solution.py:26
  246.9 1.7 copy-start.1
  247.0 1.7 copy-start.6
  250.2 5.6 %collective-permute-start = (bf16[3,256]{0,1:T(8,128)(2,1)S(1)}, bf16[3,256]{0,1:T(8,128)(2,1)S(1)}, u32[]{:S(2)}, u32[]{:S(2)}) collective-permute-start(bf16[3,256]{0,1:T(8,128)(2,1)S(1)} %get-tuple-element.164), channel_id=1, source_target_pairs={{0,16},{16,32},{32,48},{48,64},{64,80},{80,96},{96,112},{112,128},... | collective-permute-start | bytes 4616 | tf_op jit(solution)/shard_map/ppermute | solution.py:20
  252.2 5.9 %collective-permute-start.1 = (bf16[3,2,128]{0,2,1:T(8,128)(2,1)S(1)}, bf16[3,2,128]{0,2,1:T(8,128)(2,1)S(1)}, u32[]{:S(2)}, u32[]{:S(2)}) collective-permute-start(bf16[3,2,128]{0,2,1:T(8,128)(2,1)S(1)} %bitcast.94), channel_id=1, source_target_pairs={{0,16},{16,32},{32,48},{48,64},{64,80},{80,96},{96,112},{112,128},... | collective-permute-start | bytes 4616 | tf_op jit(solution)/shard_map/ppermute | solution.py:20
  400.2 5.2 %copy-start = (f32[16,4,128,64]{3,2,1,0:T(8,128)S(1)}, f32[16,4,128,64]{3,2,1,0:T(8,128)}, u32[]{:S(2)}) copy-start(f32[16,4,128,64]{3,2,1,0:T(8,128)} %get-tuple-element.77) | copy-start | bytes 6291460
  400.2 5.2 %copy-start.2 = (f32[16,4,64,128]{3,2,1,0:T(8,128)S(1)}, f32[16,4,64,128]{3,2,1,0:T(8,128)}, u32[]{:S(2)}) copy-start(f32[16,4,64,128]{3,2,1,0:T(8,128)} %fusion.18) | copy-start | bytes 6291460
  411.8 5.5 %collective-permute-start.2 = (f32[2048]{0:T(1024)S(1)}, f32[2048]{0:T(1024)S(1)}, u32[]{:S(2)}, u32[]{:S(2)}) collective-permute-start(f32[2048]{0:T(1024)S(1)} %get-tuple-element.160), channel_id=1, source_target_pairs={{0,1},{1,0},{2,3},{3,2},{4,5},{5,4},{6,7},{7,6},{8,9},{9,8},{10,11... | collective-permute-start | bytes 24584 | tf_op jit(solution)/shard_map/ppermute | solution.py:46
  417.4 7.0 %collective-permute-start.3 = (f32[2048]{0:T(1024)S(1)}, f32[2048]{0:T(1024)S(1)}, u32[]{:S(2)}, u32[]{:S(2)}) collective-permute-start(f32[2048]{0:T(1024)S(1)} %add.124), channel_id=1, source_target_pairs={{0,2},{1,3},{2,0},{3,1},{4,6},{5,7},{6,4},{7,5},{8,10},{9,11},{10,... | collective-permute-start | bytes 24584 | tf_op jit(solution)/shard_map/ppermute | solution.py:46
Sparse Core Ops, SparseCore 0:
  9.5 69.3 all-gather.7
  81.9 65.2 all-gather.9
  150.3 85.8 all-gather.11
  294.5 71.2 all-gather.13
where the time goes:
time: 458 us; the launch traced here: 456 us
  waiting for transfers between devices  186 us (41%)
  blocking collectives  125 us (27%)
  local copies, waits for them, and re-layouts  48.5 us (11%)
  other arithmetic  41.3 us (9%)
  matrix products  26.4 us (6%)
  between operations  14.2 us (3%)
  starting transfers between devices  12.4 us (3%)
    all_gather x1, waiting for transfers between devices, on_device(): lax.all_gather(tokens, 'inner', axis=0, tiled=True)  85.3 us
    all_gather x1, waiting for transfers between devices, on_device(): full_cols = lax.all_gather(state_rows, 'inner', axis=2, tiled=True)  66.3 us
    unnamed x1, blocking collectives  42.4 us
    all_gather x1, blocking collectives, on_device(): lax.all_gather(state_weight, 'ctx', axis=0, tiled=True)  30.7 us
    dynamic_slice x60, local copies, waits for them, and re-layouts, one(): lax.dynamic_index_in_dim(a, turn, 0, False).astype(own.dtype)  29.4 us
    all_gather x1, blocking collectives, on_device(): lax.all_gather(step_weight, 'ctx', axis=0, tiled=True)  29.1 us
    all_to_all x1, blocking collectives, on_device(): lax.all_to_all(normed, 'inner', split_axis=0, concat_axis=1, tiled=True)  23.1 us
    all_gather x1, waiting for transfers between devices, entering(): lax.all_gather(a.astype(kind), axis)  22.2 us
  transfers between devices with their start and end apart: 8, of which 7 were waited for; matrix products, arithmetic and copies ran while one was open for 4% of the time, Pallas kernels for 0%

commit v1 on v0

v1 whole, which is shorter than its diff:
```python
import functools

import jax
import jax.numpy as jnp
from jax import lax
from jax.experimental import pallas as pl
from jax.experimental.pallas import tpu as pltpu
from jax.sharding import PartitionSpec as P

H = 64
P_SIZE = 64
N = 128
G = 4
CONV = 4
SPAN = 128
EPSILON = 1e-05
MESH = pl.DeviceIdType.MESH
CTX = 32
INNER = 16
SIDE = 4
QUARTERS = 4
VMEM_LIMIT = 60 * 1024 * 1024


def remote(src, dst, send_sem, recv_sem, device):
    return pltpu.make_async_remote_copy(
        src_ref=src,
        dst_ref=dst,
        send_sem=send_sem,
        recv_sem=recv_sem,
        device_id=device,
        device_id_type=MESH,
    )


def landed(ref, sem):
    pltpu.make_async_copy(ref, ref, sem).wait()


def gather_kernel(
    tok_ref,
    project_ref,
    state_ref,
    step_ref,
    out_ref,
    tokens,
    w_project,
    w_rest,
    parts,
    tok_send,
    tok_recv,
    wp_send,
    wp_recv,
    wr_send,
    wr_recv,
    part_send,
    part_recv,
):
    ctx = lax.axis_index("ctx")
    inner = lax.axis_index("inner")
    y, x = inner // SIDE, inner % SIDE
    rows_here = project_ref.shape[0]
    other = ctx + 1 - 2 * (ctx % 2)
    up, down = (ctx + 2) % CTX, (ctx + CTX - 2) % CTX

    def at(dy, dx):
        return ((y + dy) % SIDE) * SIDE + (x + dx) % SIDE

    barrier = pltpu.get_barrier_semaphore()

    def greet(step, carry):
        pl.semaphore_signal(
            barrier, inc=1, device_id={"inner": (inner + step) % INNER}, device_id_type=MESH
        )
        return carry

    lax.fori_loop(1, INNER, greet, 0)
    for peer in (up, down, other):
        pl.semaphore_signal(barrier, inc=1, device_id={"ctx": peer}, device_id_type=MESH)
    pl.semaphore_wait(barrier, INNER - 1 + 3)

    def part_copy(step):
        to = (inner + step) % INNER
        return remote(
            state_ref.at[to // (INNER // G)],
            parts.at[inner],
            part_send,
            part_recv,
            {"inner": to},
        )

    def send_part(step, carry):
        part_copy(step).start()
        return carry

    lax.fori_loop(1, INNER, send_part, 0)
    parts[inner] = state_ref[inner // (INNER // G)]

    def rows_of(place):
        return pl.ds(pl.multiple_of(place * rows_here, rows_here), rows_here)

    def wp_copy(place, to):
        return remote(
            w_project.at[rows_of(place)],
            w_project.at[rows_of(place)],
            wp_send,
            wp_recv.at[place],
            {"ctx": to},
        )

    def wr_copy(place, to):
        return remote(
            w_rest.at[rows_of(place)],
            w_rest.at[rows_of(place)],
            wr_send,
            wr_recv.at[place],
            {"ctx": to},
        )

    w_project[rows_of(ctx)] = project_ref[...]
    for peer in (up, down, other):
        wp_copy(ctx, peer).start()

    quarter = tok_ref.shape[0] // QUARTERS

    def tok_send_to(q, held, move):
        rows = pl.ds(q * quarter, quarter)
        (dy, dx), (ay, ax) = held, move
        slot = ((dy - ay) % SIDE) * SIDE + (dx - ax) % SIDE
        mine = (dy % SIDE) * SIDE + dx % SIDE
        source = tok_ref.at[rows] if mine == 0 else tokens.at[mine, rows]
        remote(
            source,
            tokens.at[slot, rows],
            tok_send,
            tok_recv.at[q * INNER + slot],
            {"inner": at(ay, ax)},
        ).start()

    def tok_wait(q, held):
        slot = (held[0] % SIDE) * SIDE + held[1] % SIDE
        landed(tokens.at[slot, pl.ds(q * quarter, quarter)], tok_recv.at[q * INNER + slot])

    def turn(q, along, across):
        return (across, along) if q < 2 else (along, across)

    def sense(q):
        return 1 if q % 2 == 0 else -1

    for first in (True, False):
        for q in range(QUARTERS):
            for d in (sense(q), -sense(q)):
                tok_send_to(q, (0, 0), turn(q, d, 0) if first else turn(q, 0, d))
    tokens[0] = tok_ref[...]

    landed(parts.at[pl.ds(0, INNER - 1)], part_recv)
    width = 2 * N
    source_row = lax.broadcasted_iota(jnp.int32, (width, width), 0)
    target = lax.broadcasted_iota(jnp.int32, (width, width), 1)
    piece = N // INNER
    goes = (
        ((source_row // piece) % 2) * N + (source_row // (2 * piece)) * piece + source_row % piece
    )
    place = jnp.where(goes == target, 1.0, 0.0).astype(jnp.bfloat16)
    state_cols = lax.dot_general(
        parts[...].reshape(width, rows_here),
        place,
        (((0,), (0,)), ((), ())),
        preferred_element_type=jnp.float32,
    ).astype(jnp.bfloat16)
    w_rest[rows_of(ctx), :width] = state_cols
    w_rest[rows_of(ctx), width:] = step_ref[...]
    for peer in (up, down, other):
        wr_copy(ctx, peer).start()

    def relay(copy, recv, ref, hop):
        behind, ahead = (ctx + CTX - 2 * hop) % CTX, (ctx + 2 * hop) % CTX
        landed(ref.at[rows_of(behind)], recv.at[behind])
        if hop < CTX // 4:
            copy(behind, up).start()
        copy(behind, other).start()
        if hop < CTX // 4:
            landed(ref.at[rows_of(ahead)], recv.at[ahead])
            if hop < CTX // 4 - 1:
                copy(ahead, down).start()
            copy(ahead, other).start()

    def w_relay(hop):
        relay(wp_copy, wp_recv, w_project, hop)
        relay(wr_copy, wr_recv, w_rest, hop)

    def arrive(q, along, across):
        d = sense(q)
        held = turn(q, along, across)
        tok_wait(q, held)
        if across == 0:
            if along == -d:
                tok_send_to(q, held, turn(q, d, 0))
            for e in (d, -d):
                tok_send_to(q, held, turn(q, 0, e))
        elif across == -d:
            tok_send_to(q, held, turn(q, 0, d))

    for q in range(QUARTERS):
        arrive(q, -sense(q), 0)
        arrive(q, sense(q), 0)
        if q % 2:
            w_relay(1 + q // 2)
    for q in range(QUARTERS):
        arrive(q, 2, 0)
        arrive(q, 0, -sense(q))
        if q % 2:
            w_relay(3 + q // 2)
    for step in (-1, 1):
        for q in range(QUARTERS):
            arrive(q, step * sense(q), -sense(q))
        w_relay(5 + (step + 1) // 2)
    for q in range(QUARTERS):
        arrive(q, 2, -sense(q))
    w_relay(7)
    w_relay(8)

    def handed(hop, carry):
        src = (other + 2 * hop) % CTX
        landed(w_project.at[rows_of(src)], wp_recv.at[src])
        landed(w_rest.at[rows_of(src)], wr_recv.at[src])
        return carry

    lax.fori_loop(0, CTX // 2, handed, 0)

    rest_width = w_rest.shape[1]
    project_width = w_project.shape[1]
    span = tok_ref.shape[0]
    done = set()
    for q in range(QUARTERS):
        for along, across in ((-1, 0), (1, 0), (2, 0)):
            done.add((q,) + tuple(v % SIDE for v in turn(q, along, across)))
        for along in range(SIDE):
            done.add((q,) + tuple(v % SIDE for v in turn(q, along, -sense(q))))
    for dy in (0, 1, 3, 2):
        for dx in range(SIDE):
            for q in range(QUARTERS):
                if (dy, dx) != (0, 0) and (q, dy, dx) not in done:
                    tok_wait(q, (dy, dx))

        def multiply(pair, carry, dy=dy):
            first = dy * SIDE + 2 * pair
            rows = tokens[pl.ds(first, 2)].reshape(2 * span, tokens.shape[2])
            wide = jnp.dot(rows, w_project[...], preferred_element_type=jnp.float32).astype(
                jnp.bfloat16
            )
            rest = jnp.dot(rows, w_rest[...], preferred_element_type=jnp.float32).astype(
                jnp.bfloat16
            )
            for half in range(2):
                src = at(dy, 2 * pair + half)
                to = pl.ds(pl.multiple_of(src * span, span), span)
                out_ref[to, :project_width] = wide[half * span : (half + 1) * span]
                out_ref[to, project_width:] = rest[half * span : (half + 1) * span]
            return carry

        lax.fori_loop(0, 2, multiply, 0)

    landed(tokens.at[pl.ds(0, INNER - 1)], tok_send)
    landed(parts.at[pl.ds(0, INNER - 1)], part_send)
    sent = rows_here * (2 + 1 + 7 + 6 + 15)
    landed(w_project.at[pl.ds(0, sent)], wp_send)
    landed(w_rest.at[pl.ds(0, sent)], wr_send)


def gather_project(tokens, project, state, step):
    span, model = tokens.shape
    rows_here, project_width = project.shape
    rest_width = 2 * N + step.shape[1]
    total = span * INNER
    flops = 2 * total * model * (project_width + rest_width)
    return pl.pallas_call(
        gather_kernel,
        out_shape=jax.ShapeDtypeStruct((total, project_width + rest_width), jnp.bfloat16),
        in_specs=[pl.BlockSpec(memory_space=pltpu.VMEM)] * 4,
        out_specs=pl.BlockSpec(memory_space=pltpu.VMEM),
        scratch_shapes=[
            pltpu.VMEM((INNER, span, model), jnp.bfloat16),
            pltpu.VMEM((rows_here * CTX, project_width), jnp.bfloat16),
            pltpu.VMEM((rows_here * CTX, rest_width), jnp.bfloat16),
            pltpu.VMEM((INNER, 2 * N // INNER, rows_here), jnp.bfloat16),
            pltpu.SemaphoreType.DMA,
            pltpu.SemaphoreType.DMA((QUARTERS * INNER,)),
            pltpu.SemaphoreType.DMA,
            pltpu.SemaphoreType.DMA((CTX,)),
            pltpu.SemaphoreType.DMA,
            pltpu.SemaphoreType.DMA((CTX,)),
            pltpu.SemaphoreType.DMA,
            pltpu.SemaphoreType.DMA,
        ],
        compiler_params=pltpu.CompilerParams(
            collective_id=0, has_side_effects=True, vmem_limit_bytes=VMEM_LIMIT
        ),
        cost_estimate=pl.CostEstimate(flops=flops, bytes_accessed=8 * 2**20, transcendentals=0),
        name="gather_project",
    )(tokens, project, state, step)


def lane_pair(values, first):
    width = 2 * P_SIZE
    low = lax.broadcasted_iota(jnp.int32, (values.shape[0], width), 1) < P_SIZE
    return jnp.where(low, values[:, first : first + 1], values[:, first + 1 : first + 2])


def per_channel(values, heads):
    return jnp.concatenate([lane_pair(values, h) for h in range(0, heads, 2)], axis=1)


def scan_kernel(
    heads,
    pre_ref,
    taps_ref,
    bias_ref,
    rate_ref,
    gain_ref,
    out_ref,
    tail,
    active,
    cums,
    steps,
    fresh,
    logs,
    diag,
    own_state,
    own_decay,
    in_state,
    in_decay,
    back,
    prior,
    gated,
    got,
    tail_send,
    tail_recv,
    decay_send,
    decay_recv,
    state_send,
    state_recv,
    back_send,
    back_recv,
    out_send,
    out_recv,
):
    ctx = lax.axis_index("ctx")
    inner = lax.axis_index("inner")
    width = heads * P_SIZE
    blocks = pre_ref.shape[0] // SPAN
    slices = CTX // 2
    piece = N * width // slices // (2 * P_SIZE)
    halves = width // (2 * P_SIZE)
    per_half = slices // halves
    z = ctx // 2
    scans = (ctx % 2) == (z % 2)

    def scanner(k):
        return 2 * k + k % 2

    barrier = pltpu.get_barrier_semaphore()

    def greet_inner(step, carry):
        pl.semaphore_signal(
            barrier, inc=1, device_id={"inner": (inner + step) % INNER}, device_id_type=MESH
        )
        return carry

    def greet_ctx(step, carry):
        pl.semaphore_signal(
            barrier, inc=1, device_id={"ctx": (ctx + step) % CTX}, device_id_type=MESH
        )
        return carry

    lax.fori_loop(1, INNER, greet_inner, 0)
    lax.fori_loop(1, CTX, greet_ctx, 0)
    pl.semaphore_wait(barrier, INNER - 1 + CTX - 1)

    conv_cols = slice(width, 2 * width + 2 * N)
    to_tail = remote(
        pre_ref.at[pl.ds((blocks - 1) * SPAN + SPAN - 16, 16), pl.ds(width, width + 2 * N)],
        tail,
        tail_send,
        tail_recv,
        {"ctx": (ctx + 1) % CTX},
    )
    to_tail.start()

    row = lax.broadcasted_iota(jnp.int32, (SPAN, SPAN), 0)
    col = lax.broadcasted_iota(jnp.int32, (SPAN, SPAN), 1)
    lower = col <= row
    ones = jnp.where(lower, 1.0, 0.0)

    def rows_of(c):
        return pl.ds(pl.multiple_of(c * SPAN, SPAN), SPAN)

    def decays(c, total):
        raw = pre_ref[rows_of(c), 2 * width + 2 * N :].astype(jnp.float32) + bias_ref[...]
        step = jnp.maximum(raw, 0.0) + jnp.log1p(jnp.exp(-jnp.abs(raw)))
        cum = jnp.dot(
            ones,
            step * rate_ref[...],
            precision=lax.Precision.HIGHEST,
            preferred_element_type=jnp.float32,
        )
        cums[c] = cum
        steps[c] = step
        logs[c] = jnp.broadcast_to(per_channel(total, heads), (8, width))
        return total + cum[SPAN - 1 :, :]

    total = lax.fori_loop(0, blocks, decays, jnp.zeros((1, SPAN), jnp.float32))
    decay_all = jnp.exp(per_channel(total, heads))
    for half in range(halves):
        own_decay[half] = jnp.broadcast_to(
            decay_all[:, half * 2 * P_SIZE : (half + 1) * 2 * P_SIZE], (8, 2 * P_SIZE)
        )

    def send_decay(k, carry):
        to = scanner(k)

        @pl.when(to != ctx)
        def _():
            remote(
                own_decay.at[k // per_half], in_decay.at[ctx], decay_send, decay_recv, {"ctx": to}
            ).start()

        return carry

    lax.fori_loop(0, slices, send_decay, 0)

    def convolve(c, previous):
        current = pre_ref[rows_of(c), conv_cols]
        extended = jnp.concatenate([previous, current], axis=0).astype(jnp.float32)
        mixed = jnp.broadcast_to(taps_ref[CONV : CONV + 1], current.shape)
        for k in range(CONV):
            begin = 16 - (CONV - 1) + k
            mixed = mixed + taps_ref[k : k + 1] * extended[begin : begin + SPAN]
        values = (mixed / (1.0 + jnp.exp(-mixed))).astype(jnp.bfloat16)
        active[rows_of(c)] = values
        cum, step = cums[c], steps[c]
        to_end = jnp.exp(cum[SPAN - 1 :] - cum) * step
        scaled = (values[:, :width].astype(jnp.float32) * per_channel(to_end, heads)).astype(
            jnp.bfloat16
        )
        fresh[c] = lax.dot_general(
            values[:, width : width + N],
            scaled,
            (((0,), (0,)), ((), ())),
            preferred_element_type=jnp.float32,
        )

    def convolve_later(c, carry):
        convolve(c, pre_ref[pl.ds(pl.multiple_of(c * SPAN - 16, 16), 16), conv_cols])
        return carry

    lax.fori_loop(1, blocks, convolve_later, 0)
    to_tail.wait_recv()
    edge = tail[...]
    convolve(0, jnp.where(ctx > 0, edge, jnp.zeros_like(edge)))

    def chain(c, state):
        added = fresh[c]
        fresh[c] = state
        return jnp.exp(per_channel(cums[c, SPAN - 1 :], heads)) * state + added

    state = lax.fori_loop(0, blocks, chain, jnp.zeros((N, width), jnp.float32))
    for half in range(halves):
        own_state[half] = state[:, half * 2 * P_SIZE : (half + 1) * 2 * P_SIZE].astype(jnp.bfloat16)

    def slice_of(k):
        return pl.ds(pl.multiple_of((k % per_half) * piece, piece), piece)

    def send_state(k, carry):
        to = scanner(k)

        @pl.when(to != ctx)
        def _():
            remote(
                own_state.at[k // per_half, slice_of(k)],
                in_state.at[ctx],
                state_send,
                state_recv,
                {"ctx": to},
            ).start()

        return carry

    lax.fori_loop(0, slices, send_state, 0)

    @pl.when(scans)
    def _():
        in_state[ctx] = own_state[z // per_half, slice_of(z)]
        in_decay[ctx] = own_decay[z // per_half]

    def inside(c, carry):
        values = active[rows_of(c)]
        cum, step = cums[c], steps[c]
        cum_rows, step_rows = cum.T, step.T
        scores = lax.dot_general(
            values[:, width + N :],
            values[:, width : width + N],
            (((1,), (1,)), ((), ())),
            preferred_element_type=jnp.float32,
        )
        lane = lax.broadcasted_iota(jnp.int32, (SPAN, 2 * P_SIZE), 1)
        for h in range(0, heads, 2):
            mixes, sides = [], []
            xs = values[:, h * P_SIZE : (h + 2) * P_SIZE]
            for side in range(2):
                at = h + side
                gap = jnp.where(lower, cum[:, at : at + 1] - cum_rows[at : at + 1], -jnp.inf)
                mix = scores * jnp.exp(gap) * step_rows[at : at + 1]
                mixes.append(mix.astype(jnp.bfloat16))
                sides.append(jnp.where((lane < P_SIZE) == (side == 0), xs, jnp.zeros_like(xs)))
            diag[c, :, h * P_SIZE : (h + 2) * P_SIZE] = jnp.dot(
                jnp.concatenate(mixes, axis=1),
                jnp.concatenate(sides, axis=0),
                preferred_element_type=jnp.float32,
            )
        return carry

    lax.fori_loop(0, blocks, inside, 0)

    @pl.when(scans)
    def _():
        landed(in_decay.at[pl.ds(0, CTX - 1)], decay_recv)
        landed(in_state.at[pl.ds(0, CTX - 1)], state_recv)

        def join(c, running):
            back[c] = running.astype(jnp.bfloat16)

            @pl.when(c != ctx)
            def _():
                remote(
                    back.at[c], prior.at[z // per_half, slice_of(z)], back_send, back_recv, {"ctx": c}
                ).start()

            return running * in_decay[c, :1] + in_state[c].astype(jnp.float32)

        lax.fori_loop(0, CTX, join, jnp.zeros((piece, 2 * P_SIZE), jnp.float32))
        prior[z // per_half, slice_of(z)] = back[ctx]
        landed(in_state.at[pl.ds(0, slices - 1)], back_recv)

    @pl.when(jnp.logical_not(scans))
    def _():
        landed(in_state.at[pl.ds(0, slices)], back_recv)

    before = jnp.concatenate([prior[half] for half in range(halves)], axis=1).astype(jnp.float32)

    def finish(turn, carry):
        c = (inner + 1 + turn) % INNER
        state_in = (fresh[c] + jnp.exp(logs[c, :1]) * before).astype(jnp.bfloat16)
        over = jnp.dot(
            active[rows_of(c), width + N :], state_in, preferred_element_type=jnp.float32
        )
        out = diag[c] + over * per_channel(jnp.exp(cums[c]), heads)
        gate = pre_ref[rows_of(c), :width].astype(jnp.float32)
        gated[c] = (out * (gate / (1.0 + jnp.exp(-gate)))).astype(jnp.bfloat16)

        @pl.when(c != inner)
        def _():
            remote(gated.at[c], got.at[inner], out_send, out_recv, {"inner": c}).start()

        return carry

    lax.fori_loop(0, INNER, finish, 0)
    got[inner] = gated[inner]
    landed(got.at[pl.ds(0, INNER - 1)], out_recv)

    share = INNER // G
    for group in range(G):
        squares = jnp.zeros((SPAN, width), jnp.float32)
        for i in range(share):
            part = got[group * share + i].astype(jnp.float32)
            squares = squares + part * part
        power = jnp.sum(squares, axis=1, keepdims=True) / (H * P_SIZE // G)
        scale = lax.rsqrt(power + EPSILON)
        for i in range(share):
            lanes = slice((group * share + i) * width, (group * share + i + 1) * width)
            part = got[group * share + i].astype(jnp.float32)
            out_ref[:, lanes] = (part * scale * gain_ref[:, lanes]).astype(jnp.bfloat16)

    to_tail.wait_send()
    landed(gated.at[pl.ds(0, INNER - 1)], out_send)

    @pl.when(scans)
    def _():
        landed(in_decay.at[pl.ds(0, slices - 1)], decay_send)
        landed(in_state.at[pl.ds(0, slices - 1)], state_send)
        landed(back.at[pl.ds(0, CTX - 1)], back_send)

    @pl.when(jnp.logical_not(scans))
    def _():
        landed(in_decay.at[pl.ds(0, slices)], decay_send)
        landed(in_state.at[pl.ds(0, slices)], state_send)


def scan_gate(pre, taps, bias, rate, gain, heads):
    total = pre.shape[0]
    blocks = total // SPAN
    width = heads * P_SIZE
    slices = CTX // 2
    halves = width // (2 * P_SIZE)
    piece = N * width // slices // (2 * P_SIZE)
    vmem = pltpu.VMEM
    dma = pltpu.SemaphoreType.DMA
    return pl.pallas_call(
        functools.partial(scan_kernel, heads),
        out_shape=jax.ShapeDtypeStruct((total // INNER, INNER * width), jnp.bfloat16),
        in_specs=[pl.BlockSpec(memory_space=vmem)] * 5,
        out_specs=pl.BlockSpec(memory_space=vmem),
        scratch_shapes=[
            vmem((16, width + 2 * N), jnp.bfloat16),
            vmem((total, width + 2 * N), jnp.bfloat16),
            vmem((blocks, SPAN, SPAN), jnp.float32),
            vmem((blocks, SPAN, SPAN), jnp.float32),
            vmem((blocks, N, width), jnp.float32),
            vmem((blocks, 8, width), jnp.float32),
            vmem((blocks, SPAN, width), jnp.float32),
            vmem((halves, N, 2 * P_SIZE), jnp.bfloat16),
            vmem((halves, 8, 2 * P_SIZE), jnp.float32),
            vmem((CTX, piece, 2 * P_SIZE), jnp.bfloat16),
            vmem((CTX, 8, 2 * P_SIZE), jnp.float32),
            vmem((CTX, piece, 2 * P_SIZE), jnp.bfloat16),
            vmem((halves, N, 2 * P_SIZE), jnp.bfloat16),
            vmem((INNER, SPAN, width), jnp.bfloat16),
            vmem((INNER, SPAN, width), jnp.bfloat16),
        ]
        + [dma] * 10,
        compiler_params=pltpu.CompilerParams(
            collective_id=1, has_side_effects=True, vmem_limit_bytes=VMEM_LIMIT
        ),
        name="scan_gate",
    )(pre, taps, bias, rate, gain)


def pick_group(values, group):
    shaped = values.reshape(values.shape[:-1] + (N, G))
    return lax.dynamic_index_in_dim(shaped, group, shaped.ndim - 1, keepdims=False)


def on_device(
    tokens,
    project_weight,
    state_weight,
    step_weight,
    mixer_taps,
    state_taps,
    step_bias,
    decay_log,
    norm_gain,
):
    heads = step_weight.shape[1]
    group = lax.axis_index("inner") * heads // (H // G)
    rows_here = project_weight.shape[0]
    wide = project_weight.reshape(rows_here, -1)
    state = state_weight.reshape(rows_here, 2, -1, G).transpose(3, 1, 2, 0)
    state = state.reshape(G, -1, rows_here)
    step = jnp.pad(step_weight, ((0, 0), (0, SPAN - heads)))
    pre = gather_project(tokens, wide, state, step)
    taps = jnp.concatenate(
        [mixer_taps, pick_group(state_taps, group).reshape(CONV + 1, 2 * N)], axis=1
    )
    bias = jnp.pad(step_bias, (0, SPAN - heads))[None]
    rate = jnp.pad(-jnp.exp(decay_log), (0, SPAN - heads))[None]
    return scan_gate(pre, taps, bias, rate, norm_gain[None], heads)


def solution(mesh):
    placed = (
        P(("ctx", "inner"), None),
        P("ctx", None, "inner"),
        P("ctx", None, "inner"),
        P("ctx", "inner"),
        P(None, "inner"),
        P(),
        P("inner"),
        P("inner"),
        P(),
    )
    return jax.shard_map(
        on_device, mesh=mesh, in_specs=placed, out_specs=P(("ctx", "inner"), None), check_vma=False
    )
```

time: 458 us -> 140 us (0.31)
  the two profiles are of different devices: /device:TPU:480 before, /device:TPU:1 now
where the time goes in v1:
time: 140 us; the launch traced here: 139 us
  Pallas kernels  128 us (91%)
  local copies, waits for them, and re-layouts  9.57 us (7%)
  other arithmetic  1.96 us (1%)
    pallas_call x1, Pallas kernels, gather_project(): pl.pallas_call(gather_kernel, out_shape=jax.ShapeDtypeStruct((total, proj...  74.5 us
    pallas_call x1, Pallas kernels, scan_gate(): pl.pallas_call(functools.partial(scan_kernel, heads), out_shape=jax.Shape...  53.2 us
    unnamed x4, local copies, waits for them, and re-layouts  4.55 us

profile of v1, /device:TPU:1, one launch (start us, length us, event | category | flops | bytes accessed | tf_op | source)
XLA Modules:
  0.0 139.2 jit_solution(9339063291534830917)
XLA Ops:
  0.0 0.7 exponential_negate_fusion
  0.7 1.2 pad_bitcast_fusion
  1.9 1.3 copy.21
  3.2 0.8 copy.16
  4.0 0.6 pad.11.step_ref
  4.6 1.5 %copy.17 = bf16[8,8,2,256]{3,1,2,0:T(8,128)(2,1)} copy(bf16[8,8,2,256]{3,2,1,0:T(2,128)(2,1)} %bitcast.17) | data formatting | bytes 131072
  6.1 1.4 reshape.19
  7.5 0.5 dynamic-slice_reduce_fusion
  8.0 1.3 pad_maximum_fusion.taps_ref
  9.3 74.5 %gather_project.1.pre_ref = bf16[2048,896]{1,0:T(8,128)(2,1)} custom-call(bf16[128,2048]{1,0:T(8,128)(2,1)} %tok_ref.1, bf16[64,512]{1,0:T(8,128)(2,1)} %bitcast.18, bf16[4,16,64]{2,1,0:T(8,128)(2,1)} %bitcast.23, bf16[64,128]{1,0:T(8,128)(2,1)} %pad.11.step_ref), custom_call_target="tpu_custom_call" | custom-call | flops 7516192768 | bytes 8388608 | tf_op jit(solution)/shard_map/gather_project/pallas_call | solution.py:277
  83.7 53.2 %scan_gate.1 = bf16[128,4096]{1,0:T(8,128)(2,1)} custom-call(bf16[2048,896]{1,0:T(8,128)(2,1)} %gather_project.1.pre_ref, f32[5,512]{1,0:T(8,128)} %pad_maximum_fusion.taps_ref, f32[1,128]{1,0:T(1,128)} %get-tuple-element.6.bias_ref, f32[1,128]{1,0:T(1,128)} %get-tuple-element.5.rate_ref, f32[1,4096]{1,0:T(1,128)} %bitcast.21), custom_call_target="tpu_custom_call" | custom-call | tf_op jit(solution)/shard_map/scan_gate/pallas_call | solution.py:608
  136.9 2.3 %copy.24 = bf16[128,4096]{1,0:T(8,128)(2,1)} copy(bf16[128,4096]{1,0:T(8,128)(2,1)} %scan_gate.1) | data formatting | bytes 2097152
  (1 shorter events, 0.0 us)

commit v2 on v1

v2 whole, which is shorter than its diff:
```python
import functools

import jax
import jax.numpy as jnp
from jax import lax
from jax.experimental import pallas as pl
from jax.experimental.pallas import tpu as pltpu
from jax.sharding import PartitionSpec as P

H = 64
P_SIZE = 64
N = 128
G = 4
CONV = 4
SPAN = 128
EPSILON = 1e-05
MESH = pl.DeviceIdType.MESH
CTX = 32
INNER = 16
SIDE = 4
QUARTERS = 4
VMEM_LIMIT = 60 * 1024 * 1024


def remote(src, dst, send_sem, recv_sem, device):
    return pltpu.make_async_remote_copy(
        src_ref=src,
        dst_ref=dst,
        send_sem=send_sem,
        recv_sem=recv_sem,
        device_id=device,
        device_id_type=MESH,
    )


def landed(ref, sem):
    pltpu.make_async_copy(ref, ref, sem).wait()


def mixer_kernel(
    heads,
    tok_ref,
    project_ref,
    state_ref,
    step_ref,
    mixer_ref,
    maps_ref,
    bias_ref,
    decay_ref,
    got,
    tokens,
    w_project,
    w_rest,
    pieces,
    parts,
    pre,
    taps,
    lead,
    tail,
    active,
    cums,
    steps,
    logs,
    fresh,
    diag,
    scaled_c,
    opened,
    own_state,
    in_state,
    back,
    prior,
    gated,
    tok_send,
    tok_recv,
    wp_send,
    wp_recv,
    wr_send,
    wr_recv,
    part_send,
    part_recv,
    tail_send,
    tail_recv,
    state_send,
    state_recv,
    back_send,
    back_recv,
    out_send,
    out_recv,
):
    ctx = lax.axis_index("ctx")
    inner = lax.axis_index("inner")
    y, x = inner // SIDE, inner % SIDE
    rows_here = project_ref.shape[0]
    group = inner // (INNER // G)
    width = heads * P_SIZE
    other = ctx + 1 - 2 * (ctx % 2)
    up, down = (ctx + 2) % CTX, (ctx + CTX - 2) % CTX

    def at(dy, dx):
        return ((y + dy) % SIDE) * SIDE + (x + dx) % SIDE

    barrier = pltpu.get_barrier_semaphore()

    def greet(step, carry):
        pl.semaphore_signal(
            barrier, inc=1, device_id={"inner": (inner + step) % INNER}, device_id_type=MESH
        )
        return carry

    lax.fori_loop(1, INNER, greet, 0)
    for peer in (up, down, other):
        pl.semaphore_signal(barrier, inc=1, device_id={"ctx": peer}, device_id_type=MESH)
    pl.semaphore_wait(barrier, INNER - 1 + 3)

    def one_hot(index, target):
        return jnp.where(index == target, 1.0, 0.0).astype(jnp.bfloat16)

    own_cols = state_ref.shape[0] * state_ref.shape[1]
    piece = N // INNER
    row = lax.broadcasted_iota(jnp.int32, (own_cols, own_cols), 0)
    col = lax.broadcasted_iota(jnp.int32, (own_cols, own_cols), 1)
    held = (row // piece % 2) * (own_cols // 2) + (row % piece) * G + row // (2 * piece)
    sorted_cols = jnp.dot(
        one_hot(held, col),
        state_ref[...].reshape(own_cols, rows_here),
        preferred_element_type=jnp.float32,
    ).astype(jnp.bfloat16)
    pieces[...] = sorted_cols.reshape(G, 2 * piece, rows_here)

    def part_copy(step):
        to = (inner + step) % INNER
        return remote(
            pieces.at[to // (INNER // G)],
            parts.at[inner],
            part_send,
            part_recv,
            {"inner": to},
        )

    def send_part(step, carry):
        part_copy(step).start()
        return carry

    lax.fori_loop(1, INNER, send_part, 0)
    parts[inner] = pieces[group]

    def rows_of(place):
        return pl.ds(pl.multiple_of(place * rows_here, rows_here), rows_here)

    def wp_copy(place, to):
        return remote(
            w_project.at[rows_of(place)],
            w_project.at[rows_of(place)],
            wp_send,
            wp_recv.at[place],
            {"ctx": to},
        )

    def wr_copy(place, to):
        return remote(
            w_rest.at[rows_of(place)],
            w_rest.at[rows_of(place)],
            wr_send,
            wr_recv.at[place],
            {"ctx": to},
        )

    w_project[rows_of(ctx), :width] = project_ref[:, 0, :]
    w_project[rows_of(ctx), width:] = project_ref[:, 1, :]
    for peer in (up, down, other):
        wp_copy(ctx, peer).start()

    quarter = tok_ref.shape[0] // QUARTERS

    def tok_send_to(q, held, move):
        rows = pl.ds(q * quarter, quarter)
        (dy, dx), (ay, ax) = held, move
        slot = ((dy - ay) % SIDE) * SIDE + (dx - ax) % SIDE
        mine = (dy % SIDE) * SIDE + dx % SIDE
        source = tok_ref.at[rows] if mine == 0 else tokens.at[mine, rows]
        remote(
            source,
            tokens.at[slot, rows],
            tok_send,
            tok_recv.at[q * INNER + slot],
            {"inner": at(ay, ax)},
        ).start()

    def tok_wait(q, held):
        slot = (held[0] % SIDE) * SIDE + held[1] % SIDE
        landed(tokens.at[slot, pl.ds(q * quarter, quarter)], tok_recv.at[q * INNER + slot])

    def turn(q, along, across):
        return (across, along) if q < 2 else (along, across)

    def sense(q):
        return 1 if q % 2 == 0 else -1

    for first in (True, False):
        for q in range(QUARTERS):
            for d in (sense(q), -sense(q)):
                tok_send_to(q, (0, 0), turn(q, d, 0) if first else turn(q, 0, d))
    tokens[0] = tok_ref[...]

    landed(parts.at[pl.ds(0, INNER - 1)], part_recv)
    row = lax.broadcasted_iota(jnp.int32, (2 * N, 2 * N), 0)
    col = lax.broadcasted_iota(jnp.int32, (2 * N, 2 * N), 1)
    goes = (row // piece % 2) * N + (row // (2 * piece)) * piece + row % piece
    state_cols = lax.dot_general(
        parts[...].reshape(2 * N, rows_here),
        one_hot(goes, col),
        (((0,), (0,)), ((), ())),
        preferred_element_type=jnp.float32,
    ).astype(jnp.bfloat16)
    row = lax.broadcasted_iota(jnp.int32, (heads, SPAN), 0)
    col = lax.broadcasted_iota(jnp.int32, (heads, SPAN), 1)
    step_cols = lax.dot_general(
        step_ref[...],
        one_hot(row, col),
        (((0,), (0,)), ((), ())),
        preferred_element_type=jnp.float32,
    ).astype(jnp.bfloat16)
    w_rest[rows_of(ctx), : 2 * N] = state_cols
    w_rest[rows_of(ctx), 2 * N :] = step_cols
    for peer in (up, down, other):
        wr_copy(ctx, peer).start()

    row = lax.broadcasted_iota(jnp.int32, (G * N, N), 0)
    col = lax.broadcasted_iota(jnp.int32, (G * N, N), 1)
    pick = jnp.where(row == col * G + group, 1.0, 0.0)
    taps[: CONV + 1, :width] = mixer_ref[...]
    for side in range(2):
        taps[: CONV + 1, width + side * N : width + (side + 1) * N] = jnp.dot(
            maps_ref[:, side, :],
            pick,
            precision=lax.Precision.HIGHEST,
            preferred_element_type=jnp.float32,
        )
    lanes = jnp.zeros((1, SPAN - heads), jnp.float32)
    bias = jnp.concatenate([bias_ref[...], lanes], axis=1)
    rate = jnp.concatenate([-jnp.exp(decay_ref[...]), lanes], axis=1)

    def relay(copy, recv, ref, hop):
        behind, ahead = (ctx + CTX - 2 * hop) % CTX, (ctx + 2 * hop) % CTX
        landed(ref.at[rows_of(behind)], recv.at[behind])
        if hop < CTX // 4:
            copy(behind, up).start()
        copy(behind, other).start()
        if hop < CTX // 4:
            landed(ref.at[rows_of(ahead)], recv.at[ahead])
            if hop < CTX // 4 - 1:
                copy(ahead, down).start()
            copy(ahead, other).start()

    def w_relay(hop):
        relay(wp_copy, wp_recv, w_project, hop)
        relay(wr_copy, wr_recv, w_rest, hop)

    def arrive(q, along, across):
        d = sense(q)
        held = turn(q, along, across)
        tok_wait(q, held)
        if across == 0:
            if along == -d:
                tok_send_to(q, held, turn(q, d, 0))
            for e in (d, -d):
                tok_send_to(q, held, turn(q, 0, e))
        elif across == -d:
            tok_send_to(q, held, turn(q, 0, d))

    for q in range(QUARTERS):
        arrive(q, -sense(q), 0)
        arrive(q, sense(q), 0)
        if q % 2:
            w_relay(1 + q // 2)
    for q in range(QUARTERS):
        arrive(q, 2, 0)
        arrive(q, 0, -sense(q))
        if q % 2:
            w_relay(3 + q // 2)
    for step in (-1, 1):
        for q in range(QUARTERS):
            arrive(q, step * sense(q), -sense(q))
        w_relay(5 + (step + 1) // 2)
    for q in range(QUARTERS):
        arrive(q, 2, -sense(q))
    w_relay(7)
    w_relay(8)

    def handed(hop, carry):
        src = (other + 2 * hop) % CTX
        landed(w_project.at[rows_of(src)], wp_recv.at[src])
        landed(w_rest.at[rows_of(src)], wr_recv.at[src])
        return carry

    lax.fori_loop(0, CTX // 2, handed, 0)

    project_width = w_project.shape[1]
    span = tok_ref.shape[0]
    blocks = pre.shape[0] // SPAN
    conv_cols = slice(width, 2 * width + 2 * N)
    row = lax.broadcasted_iota(jnp.int32, (SPAN, SPAN), 0)
    col = lax.broadcasted_iota(jnp.int32, (SPAN, SPAN), 1)
    lower = col <= row
    ones = jnp.where(lower, 1.0, 0.0)
    to_tail = remote(
        pre.at[pl.ds(blocks * SPAN - 16, 16), pl.ds(width, width + 2 * N)],
        tail,
        tail_send,
        tail_recv,
        {"ctx": (ctx + 1) % CTX},
    )

    def span_of(c):
        return pl.ds(pl.multiple_of(c * SPAN, SPAN), SPAN)

    def head_of(h):
        return slice(h * P_SIZE, (h + 1) * P_SIZE)

    def pair_of(h):
        return slice(h * P_SIZE, (h + 2) * P_SIZE)

    def silu(v):
        return v / (1.0 + jnp.exp(-v))

    def local(c):
        @pl.when(c == 0)
        def _():
            to_tail.wait_recv()
            edge = tail[...]
            lead[...] = jnp.where(ctx > 0, edge, jnp.zeros_like(edge))

        @pl.when(c > 0)
        def _():
            begin = pl.multiple_of(jnp.maximum(c * SPAN - 16, 0), 16)
            lead[...] = pre[pl.ds(begin, 16), conv_cols]

        raw = pre[span_of(c), 2 * width + 2 * N :].astype(jnp.float32) + bias
        step = jnp.maximum(raw, 0.0) + jnp.log1p(jnp.exp(-jnp.abs(raw)))
        cum = jnp.dot(
            ones,
            step * rate,
            precision=lax.Precision.HIGHEST,
            preferred_element_type=jnp.float32,
        )
        cums[c] = cum
        steps[c] = step
        current = pre[span_of(c), conv_cols]
        extended = jnp.concatenate([lead[...], current], axis=0).astype(jnp.float32)
        mixed = jnp.broadcast_to(taps[CONV : CONV + 1], current.shape)
        for k in range(CONV):
            begin = 16 - (CONV - 1) + k
            mixed = mixed + taps[k : k + 1] * extended[begin : begin + SPAN]
        values = silu(mixed).astype(jnp.bfloat16)
        active[span_of(c)] = values
        to_end = jnp.exp(cum[SPAN - 1 :] - cum) * step
        xs = values[:, :width].astype(jnp.float32).T.astype(jnp.bfloat16)
        bs = values[:, width : width + N].astype(jnp.float32)
        for h in range(heads):
            weighted = (bs * to_end[:, h : h + 1]).astype(jnp.bfloat16)
            fresh[c, head_of(h)] = jnp.dot(
                xs[head_of(h)], weighted, preferred_element_type=jnp.float32
            )

    def inside(c):
        values = active[span_of(c)]
        cum, step = cums[c], steps[c]
        cum_rows, step_rows = cum.T, step.T
        scores = lax.dot_general(
            values[:, width + N :],
            values[:, width : width + N],
            (((1,), (1,)), ((), ())),
            preferred_element_type=jnp.float32,
        )
        cs = values[:, width + N :].astype(jnp.float32)
        begun = jnp.exp(cum)
        lane = lax.broadcasted_iota(jnp.int32, (SPAN, 2 * P_SIZE), 1)
        for h in range(0, heads, 2):
            mixes, sides = [], []
            xs = values[:, pair_of(h)]
            for side in range(2):
                at_h = h + side
                gap = jnp.where(lower, cum[:, at_h : at_h + 1] - cum_rows[at_h : at_h + 1], -jnp.inf)
                mix = scores * jnp.exp(gap) * step_rows[at_h : at_h + 1]
                mixes.append(mix.astype(jnp.bfloat16))
                sides.append(jnp.where((lane < P_SIZE) == (side == 0), xs, jnp.zeros_like(xs)))
                scaled_c[span_of(c), at_h * N : (at_h + 1) * N] = (
                    cs * begun[:, at_h : at_h + 1]
                ).astype(jnp.bfloat16)
            diag[c, :, pair_of(h)] = jnp.dot(
                jnp.concatenate(mixes, axis=1),
                jnp.concatenate(sides, axis=0),
                preferred_element_type=jnp.float32,
            )
        opened[c] = silu(pre[span_of(c), :width].astype(jnp.float32))

    done = set()
    for q in range(QUARTERS):
        for along, across in ((-1, 0), (1, 0), (2, 0)):
            done.add((q,) + tuple(v % SIDE for v in turn(q, along, across)))
        for along in range(SIDE):
            done.add((q,) + tuple(v % SIDE for v in turn(q, along, -sense(q))))
    for dy, firsts in ((0, ()), (1, (1,)), (3, (0,)), (2, (2, 3))):
        for dx in range(SIDE):
            for q in range(QUARTERS):
                if (dy, dx) != (0, 0) and (q, dy, dx) not in done:
                    tok_wait(q, (dy, dx))

        def multiply(pair, carry, dy=dy):
            first = dy * SIDE + 2 * pair
            rows = tokens[pl.ds(first, 2)].reshape(2 * span, tokens.shape[2])
            wide = jnp.dot(rows, w_project[...], preferred_element_type=jnp.float32).astype(
                jnp.bfloat16
            )
            rest = jnp.dot(rows, w_rest[...], preferred_element_type=jnp.float32).astype(
                jnp.bfloat16
            )
            for half in range(2):
                to = span_of(at(dy, 2 * pair + half))
                pre[to, :project_width] = wide[half * span : (half + 1) * span]
                pre[to, project_width:] = rest[half * span : (half + 1) * span]
            return carry

        lax.fori_loop(0, SIDE // 2, multiply, 0)
        here = (y + dy) % SIDE

        @pl.when(here == SIDE - 1)
        def _():
            to_tail.start()

        def block_at(i, here=here, firsts=firsts):
            c = here * SIDE + 1 + i
            for n, f in enumerate(firsts):
                c = jnp.where(i == SIDE - 1 + n, ((y + f) % SIDE) * SIDE, c)
            return c

        last = len(firsts) == 2

        def work(i, carry, block_at=block_at, last=last):
            local(block_at(i))
            if not last:
                inside(block_at(i))
            return carry

        lax.fori_loop(0, SIDE - 1 + len(firsts), work, 0)

    def chain(c, carry):
        state, total = carry
        end = cums[c, SPAN - 1 :]
        logs[c] = jnp.broadcast_to(total, (8, SPAN))
        keep = jnp.exp(end)
        later = []
        for h in range(heads):
            later.append(keep[:, h : h + 1] * state[head_of(h)] + fresh[c, head_of(h)])
        fresh[c] = state
        return jnp.concatenate(later, axis=0), total + end

    state, total = lax.fori_loop(
        0, blocks, chain, (jnp.zeros((width, N), jnp.float32), jnp.zeros((1, SPAN), jnp.float32))
    )
    slices = CTX // 2
    deep = width // slices
    z = ctx // 2
    scans = (ctx % 2) == (z % 2)

    def scanner(k):
        return 2 * k + k % 2

    decay = jnp.exp(total)
    third = lax.broadcasted_iota(jnp.int32, (deep, N), 0)
    for h in range(heads):
        whole = jnp.broadcast_to(decay[:, h : h + 1], (deep, N))
        high = whole.astype(jnp.bfloat16).astype(jnp.float32)
        middle = (whole - high).astype(jnp.bfloat16).astype(jnp.float32)
        low = whole - high - middle
        packed = jnp.where(
            third == 0, high, jnp.where(third == 1, middle, jnp.where(third == 2, low, 0.0))
        ).astype(jnp.bfloat16)
        for k in range(h * P_SIZE // deep, (h + 1) * P_SIZE // deep):
            own_state[k, :deep] = state[k * deep : (k + 1) * deep].astype(jnp.bfloat16)
            own_state[k, deep:] = packed

    def send_state(turned, carry):
        k = (z + turned) % slices
        to = scanner(k)

        @pl.when(to != ctx)
        def _():
            remote(
                own_state.at[k], in_state.at[ctx], state_send, state_recv, {"ctx": to}
            ).start()

        return carry

    lax.fori_loop(0, slices, send_state, 0)

    @pl.when(scans)
    def _():
        in_state[ctx] = own_state[z]

    def rest_inside(i, carry):
        inside(block_at(i))
        return carry

    lax.fori_loop(0, SIDE + 1, rest_inside, 0)

    @pl.when(scans)
    def _():
        landed(in_state.at[pl.ds(0, CTX - 1)], state_recv)

        def join(c, running):
            back[c] = running.astype(jnp.bfloat16)

            @pl.when(c != ctx)
            def _():
                remote(back.at[c], prior.at[z], back_send, back_recv, {"ctx": c}).start()

            came = in_state[c].astype(jnp.float32)
            keep = came[deep : deep + 1] + came[deep + 1 : deep + 2] + came[deep + 2 : deep + 3]
            return running * keep + came[:deep]

        lax.fori_loop(0, CTX, join, jnp.zeros((deep, N), jnp.float32))
        prior[z] = back[ctx]
        landed(prior.at[pl.ds(0, slices - 1)], back_recv)

    @pl.when(jnp.logical_not(scans))
    def _():
        landed(prior, back_recv)

    before = prior[...].astype(jnp.float32).reshape(width, N)
    low_rows = lax.broadcasted_iota(jnp.int32, (2 * P_SIZE, N), 0) < P_SIZE

    def finish(turned, carry):
        c = (inner + 1 + turned) % INNER
        reach = jnp.exp(logs[c, :1])
        for h in range(0, heads, 2):
            carried = jnp.where(low_rows, reach[:, h : h + 1], reach[:, h + 1 : h + 2])
            entered = fresh[c, pair_of(h)] + carried * before[pair_of(h)]
            high = entered.astype(jnp.bfloat16)
            low = (entered - high.astype(jnp.float32)).astype(jnp.bfloat16)
            over = diag[c, :, pair_of(h)]
            for share in (high, low):
                none = jnp.zeros_like(share)
                over = over + lax.dot_general(
                    scaled_c[span_of(c), h * N : (h + 2) * N],
                    jnp.concatenate(
                        [jnp.where(low_rows, share, none), jnp.where(low_rows, none, share)], axis=1
                    ),
                    (((1,), (1,)), ((), ())),
                    preferred_element_type=jnp.float32,
                )
            gated[c, :, pair_of(h)] = (over * opened[c, :, pair_of(h)]).astype(jnp.bfloat16)

        @pl.when(c != inner)
        def _():
            remote(gated.at[c], got.at[inner], out_send, out_recv, {"inner": c}).start()

        return carry

    lax.fori_loop(0, INNER, finish, 0)
    got[inner] = gated[inner]

    landed(tokens.at[pl.ds(0, INNER - 1)], tok_send)
    landed(parts.at[pl.ds(0, INNER - 1)], part_send)
    sent = rows_here * (2 + 1 + 7 + 6 + 15)
    landed(w_project.at[pl.ds(0, sent)], wp_send)
    landed(w_rest.at[pl.ds(0, sent)], wr_send)
    to_tail.wait_send()

    @pl.when(scans)
    def _():
        landed(own_state.at[pl.ds(0, slices - 1)], state_send)
        landed(back.at[pl.ds(0, CTX - 1)], back_send)

    @pl.when(jnp.logical_not(scans))
    def _():
        landed(own_state, state_send)

    landed(gated.at[pl.ds(0, INNER - 1)], out_send)
    landed(got.at[pl.ds(0, INNER - 1)], out_recv)


def norm_kernel(got, gain_ref, out_ref):
    span, width = got.shape[1], got.shape[2]
    share = INNER // G
    for group in range(G):
        squares = jnp.zeros((span, width), jnp.float32)
        for i in range(share):
            part = got[group * share + i].astype(jnp.float32)
            squares = squares + part * part
        power = jnp.sum(squares, axis=1, keepdims=True) / (share * width)
        scale = lax.rsqrt(power + EPSILON)
        for i in range(share):
            lanes = slice((group * share + i) * width, (group * share + i + 1) * width)
            part = got[group * share + i].astype(jnp.float32)
            out_ref[:, lanes] = (part * scale * gain_ref[:, lanes]).astype(jnp.bfloat16)


def on_device(
    tokens,
    project_weight,
    state_weight,
    step_weight,
    mixer_taps,
    state_taps,
    step_bias,
    decay_log,
    norm_gain,
):
    heads = step_weight.shape[1]
    rows_here = project_weight.shape[0]
    span, model = tokens.shape
    width = heads * P_SIZE
    total = span * INNER
    blocks = total // SPAN
    slices = CTX // 2
    deep = width // slices
    rest = 2 * N + SPAN
    vmem = pltpu.VMEM
    dma = pltpu.SemaphoreType.DMA
    bf16, f32 = jnp.bfloat16, jnp.float32
    got = pl.pallas_call(
        functools.partial(mixer_kernel, heads),
        out_shape=jax.ShapeDtypeStruct((INNER, span, width), bf16),
        in_specs=[pl.BlockSpec(memory_space=vmem)] * 8,
        out_specs=pl.BlockSpec(memory_space=vmem),
        scratch_shapes=[
            vmem((INNER, span, model), bf16),
            vmem((rows_here * CTX, 2 * width), bf16),
            vmem((rows_here * CTX, rest), bf16),
            vmem((G, 2 * N // INNER, rows_here), bf16),
            vmem((INNER, 2 * N // INNER, rows_here), bf16),
            vmem((total, 2 * width + rest), bf16),
            vmem((8, width + 2 * N), f32),
            vmem((16, width + 2 * N), bf16),
            vmem((16, width + 2 * N), bf16),
            vmem((total, width + 2 * N), bf16),
            vmem((blocks, SPAN, SPAN), f32),
            vmem((blocks, SPAN, SPAN), f32),
            vmem((blocks, 8, SPAN), f32),
            vmem((blocks, width, N), f32),
            vmem((blocks, SPAN, width), f32),
            vmem((total, heads * N), bf16),
            vmem((blocks, SPAN, width), f32),
            vmem((slices, 2 * deep, N), bf16),
            vmem((CTX, 2 * deep, N), bf16),
            vmem((CTX, deep, N), bf16),
            vmem((slices, deep, N), bf16),
            vmem((INNER, SPAN, width), bf16),
            dma,
            dma((QUARTERS * INNER,)),
            dma,
            dma((CTX,)),
            dma,
            dma((CTX,)),
        ]
        + [dma] * 10,
        compiler_params=pltpu.CompilerParams(
            collective_id=0, has_side_effects=True, vmem_limit_bytes=VMEM_LIMIT
        ),
        name="mixer",
    )(
        tokens,
        project_weight,
        state_weight.transpose(1, 2, 0),
        step_weight.T,
        mixer_taps,
        state_taps,
        step_bias[None],
        decay_log[None],
    )
    return pl.pallas_call(
        norm_kernel,
        out_shape=jax.ShapeDtypeStruct((span, INNER * width), bf16),
        in_specs=[pl.BlockSpec(memory_space=vmem)] * 2,
        out_specs=pl.BlockSpec(memory_space=vmem),
        name="norm",
    )(got, norm_gain[None])


def solution(mesh):
    placed = (
        P(("ctx", "inner"), None),
        P("ctx", None, "inner"),
        P("ctx", None, "inner"),
        P("ctx", "inner"),
        P(None, "inner"),
        P(),
        P("inner"),
        P("inner"),
        P(),
    )
    return jax.shard_map(
        on_device, mesh=mesh, in_specs=placed, out_specs=P(("ctx", "inner"), None), check_vma=False
    )
```

time: 140 us -> 125 us (0.89)
  local copies, waits for them, and re-layouts: 9.57 us -> 0 us
  Pallas kernels: 128 us -> 125 us
  other arithmetic: 1.96 us -> 0 us
    unnamed x4 -> x0, local copies, waits for them, and re-layouts: 4.55 us -> none
    pallas_call x2, Pallas kernels: 128 us -> 125 us  [the longest x1 122 us: on_device(): pl.pallas_call(functools.partial(mixer_kernel, heads), out_shape=jax.Shap...]
    reshape x2 -> x0, local copies, waits for them, and re-layouts: 2.71 us -> none  [the longest x1 1.39 us: pick_group(): shaped = values.reshape(values.shape[:-1] + (N, G))]
where the time goes in v2:
time: 125 us
  Pallas kernels  125 us (100%)
    pallas_call x1, Pallas kernels, on_device(): pl.pallas_call(functools.partial(mixer_kernel, heads), out_shape=jax.Shap...  122 us
    pallas_call x1, Pallas kernels, on_device(): pl.pallas_call(norm_kernel, out_shape=jax.ShapeDtypeStruct((span, INNER *...  2.62 us

profile of v2, /device:TPU:1, one launch (start us, length us, event | category | flops | bytes accessed | tf_op | source)
XLA Modules:
  0.0 124.7 jit_solution(6064751004909506208)
XLA Ops:
  0.0 122.0 %mixer.1.got = bf16[16,128,256]{2,1,0:T(8,128)(2,1)} custom-call(bf16[128,2048]{1,0:T(8,128)(2,1)} %tok_ref.1, bf16[64,2,256]{2,1,0:T(2,128)(2,1)} %project_ref.1, bf16[2,32,64]{2,1,0:T(8,128)(2,1)} %bitcast.5, bf16[4,64]{1,0:T(4,128)(2,1)} %bitcast.7, f32[5,256]{1,0:T(8,128)} %mixer_ref.1, f32[5,2,512]{2,1,0:T(2,128)} %maps_ref.1, f32[1,4]{1,0:T(1,128)} %bitcast.8, ...), custom_call_target="tpu_custom_call" | custom-call | tf_op jit(solution)/shard_map/mixer/pallas_call | solution.py:622
  122.0 2.6 %norm.1 = bf16[128,4096]{1,0:T(8,128)(2,1)} custom-call(bf16[16,128,256]{2,1,0:T(8,128)(2,1)} %mixer.1.got, f32[1,4096]{1,0:T(1,128)} %bitcast.6), custom_call_target="tpu_custom_call" | custom-call | tf_op jit(solution)/shard_map/norm/pallas_call | solution.py:672

commit v3 on v2

--- a/solution.py
+++ b/solution.py
@@ -72,6 +72,8 @@
     gated,
     tok_send,
     tok_recv,
+    wp_swap,
+    wr_swap,
     wp_send,
     wp_recv,
     wr_send,
@@ -99,6 +101,12 @@
     def at(dy, dx):
         return ((y + dy) % SIDE) * SIDE + (x + dx) % SIDE
 
+    core = ctx % 2
+    z = ctx // 2
+    depth = CTX // 2
+    way = 1 - 2 * core
+    onward = (ctx + CTX + 2 * way) % CTX
+
     barrier = pltpu.get_barrier_semaphore()
 
     def greet(step, carry):
@@ -110,11 +118,15 @@
     lax.fori_loop(1, INNER, greet, 0)
     for peer in (up, down, other):
         pl.semaphore_signal(barrier, inc=1, device_id={"ctx": peer}, device_id_type=MESH)
-    pl.semaphore_wait(barrier, INNER - 1 + 3)
 
     def one_hot(index, target):
         return jnp.where(index == target, 1.0, 0.0).astype(jnp.bfloat16)
 
+    def rows_of(place):
+        return pl.ds(pl.multiple_of(place * rows_here, rows_here), rows_here)
+
+    w_project[rows_of(ctx), :width] = project_ref[:, 0, :]
+    w_project[rows_of(ctx), width:] = project_ref[:, 1, :]
     own_cols = state_ref.shape[0] * state_ref.shape[1]
     piece = N // INNER
     row = lax.broadcasted_iota(jnp.int32, (own_cols, own_cols), 0)
@@ -126,105 +138,15 @@
         preferred_element_type=jnp.float32,
     ).astype(jnp.bfloat16)
     pieces[...] = sorted_cols.reshape(G, 2 * piece, rows_here)
-
-    def part_copy(step):
-        to = (inner + step) % INNER
-        return remote(
-            pieces.at[to // (INNER // G)],
-            parts.at[inner],
-            part_send,
-            part_recv,
-            {"inner": to},
-        )
-
-    def send_part(step, carry):
-        part_copy(step).start()
-        return carry
-
-    lax.fori_loop(1, INNER, send_part, 0)
     parts[inner] = pieces[group]
-
-    def rows_of(place):
-        return pl.ds(pl.multiple_of(place * rows_here, rows_here), rows_here)
-
-    def wp_copy(place, to):
-        return remote(
-            w_project.at[rows_of(place)],
-            w_project.at[rows_of(place)],
-            wp_send,
-            wp_recv.at[place],
-            {"ctx": to},
-        )
-
-    def wr_copy(place, to):
-        return remote(
-            w_rest.at[rows_of(place)],
-            w_rest.at[rows_of(place)],
-            wr_send,
-            wr_recv.at[place],
-            {"ctx": to},
-        )
-
-    w_project[rows_of(ctx), :width] = project_ref[:, 0, :]
-    w_project[rows_of(ctx), width:] = project_ref[:, 1, :]
-    for peer in (up, down, other):
-        wp_copy(ctx, peer).start()
-
-    quarter = tok_ref.shape[0] // QUARTERS
-
-    def tok_send_to(q, held, move):
-        rows = pl.ds(q * quarter, quarter)
-        (dy, dx), (ay, ax) = held, move
-        slot = ((dy - ay) % SIDE) * SIDE + (dx - ax) % SIDE
-        mine = (dy % SIDE) * SIDE + dx % SIDE
-        source = tok_ref.at[rows] if mine == 0 else tokens.at[mine, rows]
-        remote(
-            source,
-            tokens.at[slot, rows],
-            tok_send,
-            tok_recv.at[q * INNER + slot],
-            {"inner": at(ay, ax)},
-        ).start()
-
-    def tok_wait(q, held):
-        slot = (held[0] % SIDE) * SIDE + held[1] % SIDE
-        landed(tokens.at[slot, pl.ds(q * quarter, quarter)], tok_recv.at[q * INNER + slot])
-
-    def turn(q, along, across):
-        return (across, along) if q < 2 else (along, across)
-
-    def sense(q):
-        return 1 if q % 2 == 0 else -1
-
-    for first in (True, False):
-        for q in range(QUARTERS):
-            for d in (sense(q), -sense(q)):
-                tok_send_to(q, (0, 0), turn(q, d, 0) if first else turn(q, 0, d))
-    tokens[0] = tok_ref[...]
-
-    landed(parts.at[pl.ds(0, INNER - 1)], part_recv)
-    row = lax.broadcasted_iota(jnp.int32, (2 * N, 2 * N), 0)
-    col = lax.broadcasted_iota(jnp.int32, (2 * N, 2 * N), 1)
-    goes = (row // piece % 2) * N + (row // (2 * piece)) * piece + row % piece
-    state_cols = lax.dot_general(
-        parts[...].reshape(2 * N, rows_here),
-        one_hot(goes, col),
-        (((0,), (0,)), ((), ())),
-        preferred_element_type=jnp.float32,
-    ).astype(jnp.bfloat16)
     row = lax.broadcasted_iota(jnp.int32, (heads, SPAN), 0)
     col = lax.broadcasted_iota(jnp.int32, (heads, SPAN), 1)
-    step_cols = lax.dot_general(
+    w_rest[rows_of(ctx), 2 * N :] = lax.dot_general(
         step_ref[...],
         one_hot(row, col),
         (((0,), (0,)), ((), ())),
         preferred_element_type=jnp.float32,
     ).astype(jnp.bfloat16)
-    w_rest[rows_of(ctx), : 2 * N] = state_cols
-    w_rest[rows_of(ctx), 2 * N :] = step_cols
-    for peer in (up, down, other):
-        wr_copy(ctx, peer).start()
-
     row = lax.broadcasted_iota(jnp.int32, (G * N, N), 0)
     col = lax.broadcasted_iota(jnp.int32, (G * N, N), 1)
     pick = jnp.where(row == col * G + group, 1.0, 0.0)
@@ -239,22 +161,116 @@
     lanes = jnp.zeros((1, SPAN - heads), jnp.float32)
     bias = jnp.concatenate([bias_ref[...], lanes], axis=1)
     rate = jnp.concatenate([-jnp.exp(decay_ref[...]), lanes], axis=1)
+    tokens[0] = tok_ref[...]
+    row = lax.broadcasted_iota(jnp.int32, (2 * N, 2 * N), 0)
+    col = lax.broadcasted_iota(jnp.int32, (2 * N, 2 * N), 1)
+    goes = one_hot((row // piece % 2) * N + (row // (2 * piece)) * piece + row % piece, col)
+
+    pl.semaphore_wait(barrier, INNER - 1 + 3)
+
+    def swap(ref, sems):
+        return remote(
+            ref.at[rows_of(ctx)], ref.at[rows_of(ctx)], sems.at[0], sems.at[1], {"ctx": other}
+        )
+
+    def swapped(ref, sems):
+        landed(ref.at[rows_of(other)], sems.at[1])
+
+    def w_copy(ref, place, to, send, recv):
+        return remote(ref.at[rows_of(place)], ref.at[rows_of(place)], send, recv.at[place], {"ctx": to})
+
+    def wp_copy(place, to):
+        return w_copy(w_project, place, to, wp_send, wp_recv)
+
+    def wr_copy(place, to):
+        return w_copy(w_rest, place, to, wr_send, wr_recv)
+
+    wp_copy(ctx, onward).start()
+    swap(w_project, wp_swap).start()
+
+    def send_part(step, carry):
+        to = (inner + step) % INNER
+        remote(
+            pieces.at[to // (INNER // G)], parts.at[inner], part_send, part_recv, {"inner": to}
+        ).start()
+        return carry
+
+    lax.fori_loop(1, INNER, send_part, 0)
+
+    quarter = tok_ref.shape[0] // QUARTERS
+
+    def tok_send_to(q, held, move):
+        rows = pl.ds(q * quarter, quarter)
+        (dy, dx), (ay, ax) = held, move
+        slot = ((dy - ay) % SIDE) * SIDE + (dx - ax) % SIDE
+        mine = (dy % SIDE) * SIDE + dx % SIDE
+        source = tok_ref.at[rows] if mine == 0 else tokens.at[mine, rows]
+        remote(
+            source,
+            tokens.at[slot, rows],
+            tok_send,
+            tok_recv.at[q * INNER + slot],
+            {"inner": at(ay, ax)},
+        ).start()
+
+    def tok_wait(q, held):
+        slot = (held[0] % SIDE) * SIDE + held[1] % SIDE
+        landed(tokens.at[slot, pl.ds(q * quarter, quarter)], tok_recv.at[q * INNER + slot])
+
+    def turn(q, along, across):
+        return (across, along) if q < 2 else (along, across)
+
+    def sense(q):
+        return 1 if q % 2 == 0 else -1
+
+    for q in range(QUARTERS):
+        for d in (sense(q), -sense(q)):
+            tok_send_to(q, (0, 0), turn(q, d, 0))
+    swapped(w_project, wp_swap)
+    wp_copy(other, onward).start()
+    for q in range(QUARTERS):
+        for d in (sense(q), -sense(q)):
+            tok_send_to(q, (0, 0), turn(q, 0, d))
+
+    landed(parts.at[pl.ds(0, INNER - 1)], part_recv)
+    w_rest[rows_of(ctx), : 2 * N] = lax.dot_general(
+        parts[...].reshape(2 * N, rows_here),
+        goes,
+        (((0,), (0,)), ((), ())),
+        preferred_element_type=jnp.float32,
+    ).astype(jnp.bfloat16)
+    wr_copy(ctx, onward).start()
+    swap(w_rest, wr_swap).start()
 
     def relay(copy, recv, ref, hop):
-        behind, ahead = (ctx + CTX - 2 * hop) % CTX, (ctx + 2 * hop) % CTX
-        landed(ref.at[rows_of(behind)], recv.at[behind])
-        if hop < CTX // 4:
-            copy(behind, up).start()
-        copy(behind, other).start()
-        if hop < CTX // 4:
-            landed(ref.at[rows_of(ahead)], recv.at[ahead])
-            if hop < CTX // 4 - 1:
-                copy(ahead, down).start()
-            copy(ahead, other).start()
+        def step():
+            chip = (z + depth - way * hop) % depth
+            for place in (2 * chip + core, 2 * chip + 1 - core):
+                landed(ref.at[rows_of(place)], recv.at[place])
+                if hop < depth // 2 - 1:
+                    copy(place, onward).start()
+                elif hop == depth // 2 - 1:
+
+                    @pl.when(core == 0)
+                    def _():
+                        copy(place, onward).start()
+
+                copy(place, other).start()
+
+        if hop < depth // 2:
+            step()
+        else:
+            pl.when(core == 0)(step)
+
+    def wp_relay(hop):
+        relay(wp_copy, wp_recv, w_project, hop)
+
+    def wr_relay(hop):
+        relay(wr_copy, wr_recv, w_rest, hop)
 
     def w_relay(hop):
-        relay(wp_copy, wp_recv, w_project, hop)
-        relay(wr_copy, wr_recv, w_rest, hop)
+        wp_relay(hop)
+        wr_relay(hop)
 
     def arrive(q, along, across):
         d = sense(q)
@@ -270,30 +286,42 @@
 
     for q in range(QUARTERS):
         arrive(q, -sense(q), 0)
+    wp_relay(1)
+    swapped(w_rest, wr_swap)
+    wr_copy(other, onward).start()
+    for q in range(QUARTERS):
         arrive(q, sense(q), 0)
-        if q % 2:
-            w_relay(1 + q // 2)
+    wr_relay(1)
+    w_relay(2)
+    for q in range(QUARTERS):
+        arrive(q, 0, -sense(q))
+    w_relay(3)
     for q in range(QUARTERS):
         arrive(q, 2, 0)
-        arrive(q, 0, -sense(q))
-        if q % 2:
-            w_relay(3 + q // 2)
-    for step in (-1, 1):
-        for q in range(QUARTERS):
-            arrive(q, step * sense(q), -sense(q))
-        w_relay(5 + (step + 1) // 2)
+    w_relay(4)
+    w_relay(5)
+    for q in range(QUARTERS):
+        arrive(q, -sense(q), -sense(q))
+    w_relay(6)
+    w_relay(7)
+    for q in range(QUARTERS):
+        arrive(q, sense(q), -sense(q))
+    w_relay(8)
     for q in range(QUARTERS):
         arrive(q, 2, -sense(q))
-    w_relay(7)
-    w_relay(8)
 
     def handed(hop, carry):
-        src = (other + 2 * hop) % CTX
-        landed(w_project.at[rows_of(src)], wp_recv.at[src])
-        landed(w_rest.at[rows_of(src)], wr_recv.at[src])
+        chip = (z + depth + way * hop) % depth
+        for place in (2 * chip, 2 * chip + 1):
+            landed(w_project.at[rows_of(place)], wp_recv.at[place])
+            landed(w_rest.at[rows_of(place)], wr_recv.at[place])
         return carry
 
-    lax.fori_loop(0, CTX // 2, handed, 0)
+    lax.fori_loop(1, depth // 2, handed, 0)
+
+    @pl.when(core == 1)
+    def _():
+        handed(depth // 2, 0)
 
     project_width = w_project.shape[1]
     span = tok_ref.shape[0]
@@ -406,22 +434,17 @@
                 if (dy, dx) != (0, 0) and (q, dy, dx) not in done:
                     tok_wait(q, (dy, dx))
 
-        def multiply(pair, carry, dy=dy):
-            first = dy * SIDE + 2 * pair
-            rows = tokens[pl.ds(first, 2)].reshape(2 * span, tokens.shape[2])
-            wide = jnp.dot(rows, w_project[...], preferred_element_type=jnp.float32).astype(
-                jnp.bfloat16
-            )
-            rest = jnp.dot(rows, w_rest[...], preferred_element_type=jnp.float32).astype(
-                jnp.bfloat16
-            )
-            for half in range(2):
-                to = span_of(at(dy, 2 * pair + half))
-                pre[to, :project_width] = wide[half * span : (half + 1) * span]
-                pre[to, project_width:] = rest[half * span : (half + 1) * span]
-            return carry
-
-        lax.fori_loop(0, SIDE // 2, multiply, 0)
+        rows = tokens[dy * SIDE : (dy + 1) * SIDE].reshape(SIDE * span, tokens.shape[2])
+        for weights, first in ((w_project, 0), (w_rest, project_width)):
+            for begin in range(0, weights.shape[1], 2 * SPAN):
+                end = min(begin + 2 * SPAN, weights.shape[1])
+                product = jnp.dot(
+                    rows, weights[:, begin:end], preferred_element_type=jnp.float32
+                ).astype(jnp.bfloat16)
+                for dx in range(SIDE):
+                    pre[span_of(at(dy, dx)), first + begin : first + end] = product[
+                        dx * span : (dx + 1) * span
+                    ]
         here = (y + dy) % SIDE
 
         @pl.when(here == SIDE - 1)
@@ -460,7 +483,6 @@
     )
     slices = CTX // 2
     deep = width // slices
-    z = ctx // 2
     scans = (ctx % 2) == (z % 2)
 
     def scanner(k):
@@ -562,9 +584,20 @@
 
     landed(tokens.at[pl.ds(0, INNER - 1)], tok_send)
     landed(parts.at[pl.ds(0, INNER - 1)], part_send)
-    sent = rows_here * (2 + 1 + 7 + 6 + 15)
-    landed(w_project.at[pl.ds(0, sent)], wp_send)
-    landed(w_rest.at[pl.ds(0, sent)], wr_send)
+    landed(w_project.at[rows_of(ctx)], wp_swap.at[0])
+    landed(w_rest.at[rows_of(ctx)], wr_swap.at[0])
+
+    @pl.when(core == 0)
+    def _():
+        landed(w_project, wp_send)
+        landed(w_rest, wr_send)
+
+    @pl.when(core == 1)
+    def _():
+        fewer = pl.ds(0, (depth - 2) * 2 * rows_here)
+        landed(w_project.at[fewer], wp_send)
+        landed(w_rest.at[fewer], wr_send)
+
     to_tail.wait_send()
 
     @pl.when(scans)
@@ -649,6 +682,8 @@
             vmem((INNER, SPAN, width), bf16),
             dma,
             dma((QUARTERS * INNER,)),
+            dma((2,)),
+            dma((2,)),
             dma,
             dma((CTX,)),
             dma,

time: 125 us -> 118 us (0.944)
  Pallas kernels: 125 us -> 118 us
    pallas_call x1, Pallas kernels: 122 us -> 115 us  [on_device(): pl.pallas_call(functools.partial(mixer_kernel, heads), out_shape=jax.Shap...]
where the time goes in v3:
time: 118 us
  Pallas kernels  118 us (100%)
    pallas_call x1, Pallas kernels, on_device(): pl.pallas_call(functools.partial(mixer_kernel, heads), out_shape=jax.Shap...  115 us
    pallas_call x1, Pallas kernels, on_device(): pl.pallas_call(norm_kernel, out_shape=jax.ShapeDtypeStruct((span, INNER *...  2.62 us

profile of v3, /device:TPU:1, one launch (start us, length us, event | category | flops | bytes accessed | tf_op | source)
XLA Modules:
  0.0 117.8 jit_solution(12323525220009575338)
XLA Ops:
  0.0 115.1 %mixer.1.got = bf16[16,128,256]{2,1,0:T(8,128)(2,1)} custom-call(bf16[128,2048]{1,0:T(8,128)(2,1)} %tok_ref.1, bf16[64,2,256]{2,1,0:T(2,128)(2,1)} %project_ref.1, bf16[2,32,64]{2,1,0:T(8,128)(2,1)} %bitcast.5, bf16[4,64]{1,0:T(4,128)(2,1)} %bitcast.7, f32[5,256]{1,0:T(8,128)} %mixer_ref.1, f32[5,2,512]{2,1,0:T(2,128)} %maps_ref.1, f32[1,4]{1,0:T(1,128)} %bitcast.8, ...), custom_call_target="tpu_custom_call" | custom-call | tf_op jit(solution)/shard_map/mixer/pallas_call | solution.py:655
  115.1 2.6 %norm.1 = bf16[128,4096]{1,0:T(8,128)(2,1)} custom-call(bf16[16,128,256]{2,1,0:T(8,128)(2,1)} %mixer.1.got, f32[1,4096]{1,0:T(1,128)} %bitcast.6), custom_call_target="tpu_custom_call" | custom-call | tf_op jit(solution)/shard_map/norm/pallas_call | solution.py:707

commit v4 on v3

--- a/solution.py
+++ b/solution.py
@@ -66,7 +66,9 @@
     scaled_c,
     opened,
     own_state,
+    own_decay,
     in_state,
+    in_decay,
     back,
     prior,
     gated,
@@ -84,6 +86,8 @@
     tail_recv,
     state_send,
     state_recv,
+    decay_send,
+    decay_recv,
     back_send,
     back_recv,
     out_send,
@@ -457,12 +461,8 @@
                 c = jnp.where(i == SIDE - 1 + n, ((y + f) % SIDE) * SIDE, c)
             return c
 
-        last = len(firsts) == 2
-
-        def work(i, carry, block_at=block_at, last=last):
+        def work(i, carry, block_at=block_at):
             local(block_at(i))
-            if not last:
-                inside(block_at(i))
             return carry
 
         lax.fori_loop(0, SIDE - 1 + len(firsts), work, 0)
@@ -489,18 +489,10 @@
         return 2 * k + k % 2
 
     decay = jnp.exp(total)
-    third = lax.broadcasted_iota(jnp.int32, (deep, N), 0)
     for h in range(heads):
-        whole = jnp.broadcast_to(decay[:, h : h + 1], (deep, N))
-        high = whole.astype(jnp.bfloat16).astype(jnp.float32)
-        middle = (whole - high).astype(jnp.bfloat16).astype(jnp.float32)
-        low = whole - high - middle
-        packed = jnp.where(
-            third == 0, high, jnp.where(third == 1, middle, jnp.where(third == 2, low, 0.0))
-        ).astype(jnp.bfloat16)
-        for k in range(h * P_SIZE // deep, (h + 1) * P_SIZE // deep):
-            own_state[k, :deep] = state[k * deep : (k + 1) * deep].astype(jnp.bfloat16)
-            own_state[k, deep:] = packed
+        own_decay[h] = jnp.broadcast_to(decay[:, h : h + 1], (1, N))
+    for k in range(slices):
+        own_state[k] = state[k * deep : (k + 1) * deep].astype(jnp.bfloat16)
 
     def send_state(turned, carry):
         k = (z + turned) % slices
@@ -509,6 +501,13 @@
         @pl.when(to != ctx)
         def _():
             remote(
+                own_decay.at[k * heads // slices],
+                in_decay.at[ctx],
+                decay_send,
+                decay_recv,
+                {"ctx": to},
+            ).start()
+            remote(
                 own_state.at[k], in_state.at[ctx], state_send, state_recv, {"ctx": to}
             ).start()
 
@@ -519,15 +518,18 @@
     @pl.when(scans)
     def _():
         in_state[ctx] = own_state[z]
-
-    def rest_inside(i, carry):
-        inside(block_at(i))
+        in_decay[ctx] = own_decay[z * heads // slices]
+
+    def all_inside(c, carry):
+        inside(c)
         return carry
 
-    lax.fori_loop(0, SIDE + 1, rest_inside, 0)
+    early = blocks // 2
+    lax.fori_loop(0, early, all_inside, 0)
 
     @pl.when(scans)
     def _():
+        landed(in_decay.at[pl.ds(0, CTX - 1)], decay_recv)
         landed(in_state.at[pl.ds(0, CTX - 1)], state_recv)
 
         def join(c, running):
@@ -537,12 +539,15 @@
             def _():
                 remote(back.at[c], prior.at[z], back_send, back_recv, {"ctx": c}).start()
 
-            came = in_state[c].astype(jnp.float32)
-            keep = came[deep : deep + 1] + came[deep + 1 : deep + 2] + came[deep + 2 : deep + 3]
-            return running * keep + came[:deep]
+            return running * in_decay[c] + in_state[c].astype(jnp.float32)
 
         lax.fori_loop(0, CTX, join, jnp.zeros((deep, N), jnp.float32))
         prior[z] = back[ctx]
+
+    lax.fori_loop(early, blocks, all_inside, 0)
+
+    @pl.when(scans)
+    def _():
         landed(prior.at[pl.ds(0, slices - 1)], back_recv)
 
     @pl.when(jnp.logical_not(scans))
@@ -602,11 +607,13 @@
 
     @pl.when(scans)
     def _():
+        landed(in_decay.at[pl.ds(0, slices - 1)], decay_send)
         landed(own_state.at[pl.ds(0, slices - 1)], state_send)
         landed(back.at[pl.ds(0, CTX - 1)], back_send)
 
     @pl.when(jnp.logical_not(scans))
     def _():
+        landed(in_decay.at[pl.ds(0, slices)], decay_send)
         landed(own_state, state_send)
 
     landed(gated.at[pl.ds(0, INNER - 1)], out_send)
@@ -675,8 +682,10 @@
             vmem((blocks, SPAN, width), f32),
             vmem((total, heads * N), bf16),
             vmem((blocks, SPAN, width), f32),
-            vmem((slices, 2 * deep, N), bf16),
-            vmem((CTX, 2 * deep, N), bf16),
+            vmem((slices, deep, N), bf16),
+            vmem((heads, 1, N), f32),
+            vmem((CTX, deep, N), bf16),
+            vmem((CTX, 1, N), f32),
             vmem((CTX, deep, N), bf16),
             vmem((slices, deep, N), bf16),
             vmem((INNER, SPAN, width), bf16),
@@ -689,7 +698,7 @@
             dma,
             dma((CTX,)),
         ]
-        + [dma] * 10,
+        + [dma] * 12,
         compiler_params=pltpu.CompilerParams(
             collective_id=0, has_side_effects=True, vmem_limit_bytes=VMEM_LIMIT
         ),

time: 118 us -> 116 us (0.983)
  Pallas kernels: 118 us -> 116 us
    pallas_call x1, Pallas kernels: 115 us -> 113 us  [on_device(): pl.pallas_call(functools.partial(mixer_kernel, heads), out_shape=jax.Shap...]
where the time goes in v4:
time: 116 us
  Pallas kernels  116 us (100%)
    pallas_call x1, Pallas kernels, on_device(): pl.pallas_call(functools.partial(mixer_kernel, heads), out_shape=jax.Shap...  113 us
    pallas_call x1, Pallas kernels, on_device(): pl.pallas_call(norm_kernel, out_shape=jax.ShapeDtypeStruct((span, INNER *...  2.62 us

profile of v4, /device:TPU:1, one launch (start us, length us, event | category | flops | bytes accessed | tf_op | source)
XLA Modules:
  0.0 116.1 jit_solution(6022615479941770291)
XLA Ops:
  0.0 113.5 %mixer.1.got = bf16[16,128,256]{2,1,0:T(8,128)(2,1)} custom-call(bf16[128,2048]{1,0:T(8,128)(2,1)} %tok_ref.1, bf16[64,2,256]{2,1,0:T(2,128)(2,1)} %project_ref.1, bf16[2,32,64]{2,1,0:T(8,128)(2,1)} %bitcast.5, bf16[4,64]{1,0:T(4,128)(2,1)} %bitcast.7, f32[5,256]{1,0:T(8,128)} %mixer_ref.1, f32[5,2,512]{2,1,0:T(2,128)} %maps_ref.1, f32[1,4]{1,0:T(1,128)} %bitcast.8, ...), custom_call_target="tpu_custom_call" | custom-call | tf_op jit(solution)/shard_map/mixer/pallas_call | solution.py:662
  113.5 2.6 %norm.1 = bf16[128,4096]{1,0:T(8,128)(2,1)} custom-call(bf16[16,128,256]{2,1,0:T(8,128)(2,1)} %mixer.1.got, f32[1,4096]{1,0:T(1,128)} %bitcast.6), custom_call_target="tpu_custom_call" | custom-call | tf_op jit(solution)/shard_map/norm/pallas_call | solution.py:716

commit v5 on v4

--- a/solution.py
+++ b/solution.py
@@ -656,6 +656,7 @@
     slices = CTX // 2
     deep = width // slices
     rest = 2 * N + SPAN
+    rows = span // 4
     vmem = pltpu.VMEM
     dma = pltpu.SemaphoreType.DMA
     bf16, f32 = jnp.bfloat16, jnp.float32
@@ -716,8 +717,12 @@
     return pl.pallas_call(
         norm_kernel,
         out_shape=jax.ShapeDtypeStruct((span, INNER * width), bf16),
-        in_specs=[pl.BlockSpec(memory_space=vmem)] * 2,
-        out_specs=pl.BlockSpec(memory_space=vmem),
+        grid=(span // rows,),
+        in_specs=[
+            pl.BlockSpec((INNER, rows, width), lambda i: (0, i, 0)),
+            pl.BlockSpec((1, INNER * width), lambda i: (0, 0)),
+        ],
+        out_specs=pl.BlockSpec((rows, INNER * width), lambda i: (i, 0)),
         name="norm",
     )(got, norm_gain[None])
 

time: 116 us -> 117 us (level)
  no operation moved by 1% of the time
where the time goes in v5:
time: 117 us
  Pallas kernels  117 us (100%)
    pallas_call x1, Pallas kernels, on_device(): pl.pallas_call(functools.partial(mixer_kernel, heads), out_shape=jax.Shap...  113 us
    pallas_call x1, Pallas kernels, on_device(): pl.pallas_call(norm_kernel, out_shape=jax.ShapeDtypeStruct((span, INNER *...  3.66 us

profile of v5, /device:TPU:1, one launch (start us, length us, event | category | flops | bytes accessed | tf_op | source)
XLA Modules:
  0.0 117.1 jit_solution(16631434559043015366)
XLA Ops:
  0.0 113.5 %mixer.1.got = bf16[16,128,256]{2,1,0:T(8,128)(2,1)} custom-call(bf16[128,2048]{1,0:T(8,128)(2,1)} %tok_ref.1, bf16[64,2,256]{2,1,0:T(2,128)(2,1)} %project_ref.1, bf16[2,32,64]{2,1,0:T(8,128)(2,1)} %bitcast.5, bf16[4,64]{1,0:T(4,128)(2,1)} %bitcast.7, f32[5,256]{1,0:T(8,128)} %mixer_ref.1, f32[5,2,512]{2,1,0:T(2,128)} %maps_ref.1, f32[1,4]{1,0:T(1,128)} %bitcast.8, ...), custom_call_target="tpu_custom_call" | custom-call | tf_op jit(solution)/shard_map/mixer/pallas_call | solution.py:663
  113.5 3.7 %norm.1 = bf16[128,4096]{1,0:T(8,128)(2,1)} custom-call(bf16[16,128,256]{2,1,0:T(8,128)(2,1)} %mixer.1.got, f32[1,4096]{1,0:T(1,128)} %bitcast.6), custom_call_target="tpu_custom_call" | custom-call | tf_op jit(solution)/shard_map/norm/pallas_call | solution.py:717
